TPU v7x, 32 devices: a whole 2x2x4 slice. The times are simulated.
32 devices in a mesh: lat: 8 (over z, core), lon: 4 (over y, x).
Axes of the slice: x: 2, y: 2, z: 4, core: 2. Of those that a mesh axis runs over, the one named last changes fastest.
Arguments:
- fields: bfloat16 [512, 16, 16, 128], P(None, 'lat', 'lon'), may hold values from -6 to 6
- chan_mean: float32 [128], replicated, may hold values from -1 to 1
- chan_std: float32 [128], replicated, may hold values from 0.5 to 2
- sea_mask: int32 [512, 16, 16], P(None, 'lat', 'lon'), may hold values from 0 to 1, as said below
- missing: int32 [512, 16, 16], P(None, 'lat', 'lon'), may hold values from 0 to 1, as said below
- cotangent: bfloat16 [512, 16, 16, 128], P(None, 'lat', 'lon'), may hold values from -6 to 6
- w_master: float32 [2, 1152, 128], P(None, 'lat', 'lon'), may hold values from -0.1875 to 0.1875
- w_first: float32 [2, 1152, 128], P(None, 'lat', 'lon'), may hold values from -0.0012207031 to 0.0012207031
- w_second: float32 [2, 1152, 128], P(None, 'lat', 'lon'), may hold values from 3.3864327e-09 to 1.3545731e-08
- vec_master: float32 [3, 128], replicated, may hold values from -1 to 2.16
- vec_first: float32 [3, 128], replicated, may hold values from -0.0012207031 to 0.0012207031
- vec_second: float32 [3, 128], replicated, may hold values from 3.3864327e-09 to 1.3545731e-08
Outputs:
- block_out: bfloat16 [512, 16, 16, 128], P(None, 'lat', 'lon')
- field_grad: float32 [512, 16, 16, 128], P(None, 'lat', 'lon')
- grad_norm: float32 [], replicated
- w_new: float32 [2, 1152, 128], P(None, 'lat', 'lon')
- w_first_new: float32 [2, 1152, 128], P(None, 'lat', 'lon')
- w_second_new: float32 [2, 1152, 128], P(None, 'lat', 'lon')
- w_low: bfloat16 [2, 1152, 128], P(None, 'lat', 'lon')
- vec_new: float32 [3, 128], replicated
- vec_first_new: float32 [3, 128], replicated
- vec_second_new: float32 [3, 128], replicated
Inputs may be any that keep to these rules, and one draw needn't show every extreme that they name: `sea_mask`: 1 marks sea; in every sample the pixel in the last latitude row and last longitude column is sea. `missing`: 1 marks a pixel without data; in every sample the pixel in the last latitude row and last longitude column has data.
All inputs are finite; a program needn't handle non-finite values.
Results may differ from a plain program's by a relative error of at most 0.0053.
Values may be sent and summed in bfloat16 or wider, within the bound.
A program may use at most 128 MiB of HBM per device.

v0:
```python
import functools

import jax
import jax.numpy as jnp
from jax import lax
from jax.experimental import pallas as pl
from jax.experimental.pallas import tpu as pltpu
from jax.sharding import PartitionSpec as P

STEP = 10
EPS = 1e-05
MAX_NORM = 1.0
BETA_ONE = 0.9
BETA_TWO = 0.999
ADAM_EPS = 1e-08
RATE_KERNEL = 0.02
RATE_VECTOR = 0.1
DECAY = 0.01

MESH = pl.DeviceIdType.MESH
BF = jnp.bfloat16
F32 = jnp.float32
C = 128
R = 2
W = R * C
FIRST, SECOND = 0, 1


def cols_of(i):
    return slice(i * C, (i + 1) * C)


def twice(row):
    return jnp.concatenate([row, row], axis=1)


def fold(row):
    return row[:, :C] + row[:, C:]


def to_eight(block):
    rows, width = block.shape
    return jnp.sum(block.reshape(rows // 8, 8, width), axis=0)


def total_row(block):
    return jnp.sum(block, axis=0, keepdims=True)


def both_masks(missing, sea):
    have = (1 - missing).astype(F32)
    present = jnp.concatenate([have[0], have[1]], axis=0)
    counted = None
    if sea is not None:
        land = have * sea.astype(F32)
        counted = jnp.concatenate([land[0], land[1]], axis=0)
    return present, counted


def smooth(value):
    small = jnp.exp(-jnp.abs(value))
    one = 1.0 + small
    soft = jnp.maximum(value, 0.0) + jnp.log(one)
    sigmoid = jnp.where(value >= 0.0, 1.0, small) / one
    return 0.3 * value + 0.7 * soft, 0.3 + 0.7 * sigmoid


class Sizes:
    def __init__(self, nla, nlo, samples, quads, wrows, wcols):
        self.nla, self.nlo = nla, nlo
        self.n = nla * nlo
        self.B, self.Q = samples, quads
        self.PX = R * quads
        self.S = samples // nlo
        self.L = quads * nlo
        self.CH = self.S // 4 if self.S % 64 == 0 else 16
        self.nch = self.S // self.CH
        self.wr, self.wc = wrows, wcols
        self.LP = -(-wrows // 128) * 128


def main_kernel(
    z,
    fields, cot, sea, missing, mean, std, wt, vec,
    ob, fo, gw, gv, gn,
    fin, cin, fb, pres, cm, cnt, sb, cb,
    X, H, G, F, act, slope, sg, ct, pre, bo, fs,
    w1, w2, t1, t2, acc1, acc2,
    ws, wg, kg_in, kf, kl,
    rsb, rr, kform, ssum, ts, lb, lr,
    y1, y2, y3,
    load_sem, mask_s, mask_r, f_s, f_r, c_s, c_r, halo_s, halo_r,
    bo_s, bo_r, fo_s, fo_r, wg_s, wg_r, kz_s, kz_r, kc_s, kc_r,
    ra_s, ra_r, ro_s, ro_r, y_s, y_r,
):
    nla, nlo, n = z.nla, z.nlo, z.n
    S, L, Q, CH, nch = z.S, z.L, z.Q, z.CH, z.nch
    la = lax.axis_index("lat")
    lo = lax.axis_index("lon")
    me = la * nlo + lo

    def remote(src, dst, ss, rs, lat_to, lon_to):
        return pltpu.make_async_remote_copy(
            src, dst, ss, rs, device_id=(lat_to, lon_to), device_id_type=MESH
        )

    def loop(low, high, body):
        def step(k, carry):
            body(k)
            return carry
        lax.fori_loop(low, high, step, 0)

    def others(body):
        def row(i):
            def one(j):
                @pl.when(jnp.logical_or(i != la, j != lo))
                def _():
                    body(i, j)
            loop(0, nlo, one)
        loop(0, nla, row)

    def chunk(c):
        return pl.ds(pl.multiple_of(c * CH, CH), CH)

    def peer(k):
        return lax.rem(lo + k, nlo)

    barrier = pltpu.get_barrier_semaphore()
    others(lambda i, j: pl.semaphore_signal(barrier, inc=1, device_id=(i, j), device_id_type=MESH))
    load_f = pltpu.make_async_copy(fields, fin, load_sem.at[0])
    load_c = pltpu.make_async_copy(cot, cin, load_sem.at[1])
    load_f.start()
    load_c.start()

    present, counted = both_masks(missing[...], sea[...])
    pres[...] = present.T
    cm[lo] = counted
    pad = z.LP - z.wr
    for k in range(2):
        block = wt[k].astype(BF)
        if pad:
            block = jnp.concatenate([block, jnp.zeros((z.wc, pad), BF)], axis=1)
        ws[k] = block
        wg[lo, k] = block
    for ref in (X, H, G, F):
        @pl.when(la == 0)
        def _():
            ref[:, :, cols_of(0)] = jnp.zeros((L + 2, S, C), BF)

        @pl.when(la == nla - 1)
        def _():
            ref[:, :, cols_of(3)] = jnp.zeros((L + 2, S, C), BF)

    pl.semaphore_wait(barrier, n - 1)

    def w_copy(k):
        m = peer(k)
        return remote(ws, wg.at[lo], wg_s.at[k], wg_r.at[k], la, m)

    def mask_copy(k):
        return remote(cm.at[lo], cm.at[lo], mask_s.at[k], mask_r.at[k], la, peer(k))

    loop(1, nlo, lambda k: w_copy(k).start())
    load_f.wait()

    rstd = 1.0 / std[...]
    center_in = mean[...]

    def place(src, t, c, put, standardize):
        first = pl.multiple_of((t * S + c * CH) * z.PX, CH * z.PX)
        fb[...] = src[pl.ds(first, CH * z.PX), :].astype(F32)
        here = pres[pl.ds(pl.multiple_of(t * S + c * CH, CH), CH), :]
        for p in range(z.PX):
            value = fb[pl.ds(p, CH, stride=z.PX), :]
            if standardize:
                value = (value - center_in) * rstd * here[:, p : p + 1]
            put(p // Q, p % Q, value.astype(BF))

    def f_copy(c, k):
        return remote(
            sb.at[c, k], X.at[pl.ds(1 + Q * lo, Q), chunk(c), pl.ds(C, W)],
            f_s.at[c, k], f_r.at[c, k], la, peer(k),
        )

    def c_copy(c, k):
        return remote(
            cb.at[c, k], ct.at[pl.ds(Q * lo, Q), chunk(c), :],
            c_s.at[c, k], c_r.at[c, k], la, peer(k),
        )

    def send_fields(c):
        def one(k):
            def put(i, q, value):
                sb[c, k, q, :, cols_of(i)] = value
            place(fin, peer(k), c, put, True)
            f_copy(c, k).start()
        loop(1, nlo, one)

    def own_fields(c):
        def put(i, q, value):
            X[1 + Q * lo + q, chunk(c), cols_of(i + 1)] = value
        place(fin, lo, c, put, True)

    def own_cot(c):
        def put(i, q, value):
            ct[Q * lo + q, chunk(c), cols_of(i)] = value
        place(cin, lo, c, put, False)

    def prep_cot(c):
        def one(k):
            def put(i, q, value):
                cb[c, k, q, :, cols_of(i)] = value
            place(cin, peer(k), c, put, False)
        loop(1, nlo, one)

    loop(0, nch, send_fields)
    loop(1, nlo, lambda k: mask_copy(k).start())
    loop(0, nch, own_fields)

    loop(1, nlo, lambda k: w_copy(k).wait_recv())
    for k in range(2):
        gathered = jnp.concatenate([wg[m, k].astype(F32) for m in range(nlo)], axis=0)
        kl[k] = gathered.T[: z.wr].astype(BF)
        kg_in[k, la] = kl[k]
    core = lax.rem(la, 2)
    sibling = la + 1 - 2 * core

    def kz_copy(k, d):
        to = lax.rem(la + 2 * d, nla)
        return remote(kl.at[k], kg_in.at[k, la], kz_s.at[k, d], kz_r.at[k, d], to, lo)

    def kc_copy(k, d):
        row = lax.rem(la + nla - 2 * d, nla)
        return remote(kg_in.at[k, row], kg_in.at[k, row], kc_s.at[k, d], kc_r.at[k, d], sibling, lo)

    def start_kernel(k):
        loop(1, nla // 2, lambda d: kz_copy(k, d).start())
        kc_copy(k, 0).start()

    def forward_kernel(k):
        def one(d):
            kz_copy(k, d).wait_recv()
            kc_copy(k, d).start()
        loop(1, nla // 2, one)

    def finish_kernel(k):
        loop(0, nla // 2, lambda d: kc_copy(k, d).wait_recv())
        for i in range(nla):
            kf[pl.ds(i * z.wr, z.wr), :] = kg_in[k, i].astype(F32)

    def tap(a, b):
        return kf[pl.ds((3 * a + b) * C, C), :]

    def build_forward(ref):
        for b in range(3):
            for r in range(4):
                for i in range(R):
                    a = r - i
                    good = 0 <= a <= 2
                    block = tap(a, b).astype(BF) if good else jnp.zeros((C, C), BF)
                    ref[pl.ds((b * 4 + r) * C, C), cols_of(i)] = block

    def build_turned(ref):
        for b in range(3):
            for a in range(3):
                block = tap(2 - a, 2 - b).T.astype(BF)
                for i in range(R):
                    ref[pl.ds((b * 4 + a + i) * C, C), cols_of(i)] = block
            for i, r in ((0, 3), (1, 0)):
                ref[pl.ds((b * 4 + r) * C, C), cols_of(i)] = jnp.zeros((C, C), BF)

    start_kernel(FIRST)
    start_kernel(SECOND)

    load_c.wait()
    loop(0, nch, own_cot)
    loop(0, nch, prep_cot)
    loop(1, nlo, lambda k: mask_copy(k).wait_recv())
    rows = jnp.concatenate([cm[m] for m in range(nlo)], axis=0)
    back = z.B - lo * S
    mine = pltpu.roll(rows, lax.rem(back, z.B), 1)[:, : min(z.B, 128)].T
    for j in range(L):
        for i in range(R):
            col = (j // Q) * z.PX + i * Q + j % Q
            cnt[j, :, cols_of(i)] = jnp.broadcast_to(mine[:S, col : col + 1], (S, C))

    forward_kernel(FIRST)
    finish_kernel(FIRST)
    build_forward(w1)

    def halo_copies(ref, h, c):
        north = remote(
            ref.at[pl.ds(1, L), chunk(c), pl.ds(C, C)], ref.at[pl.ds(1, L), chunk(c), pl.ds(3 * C, C)],
            halo_s.at[h, c, 0], halo_r.at[h, c, 0], jnp.maximum(la - 1, 0), lo,
        )
        south = remote(
            ref.at[pl.ds(1, L), chunk(c), pl.ds(2 * C, C)], ref.at[pl.ds(1, L), chunk(c), pl.ds(0, C)],
            halo_s.at[h, c, 1], halo_r.at[h, c, 1], jnp.minimum(la + 1, nla - 1), lo,
        )
        return north, south

    def halo_send(ref, h, c):
        north, south = halo_copies(ref, h, c)
        pl.when(la > 0)(north.start)
        pl.when(la < nla - 1)(south.start)

    def halo_wait(ref, h, c):
        north, south = halo_copies(ref, h, c)
        pl.when(la < nla - 1)(north.wait_recv)
        pl.when(la > 0)(south.wait_recv)
        ref[0, chunk(c), :] = ref[L, chunk(c), :]
        ref[L + 1, chunk(c), :] = ref[1, chunk(c), :]

    def halo_done(ref, h, c):
        north, south = halo_copies(ref, h, c)
        pl.when(la > 0)(north.wait_send)
        pl.when(la < nla - 1)(south.wait_send)

    def taps(ref, c):
        parts = [ref[b : b + L, chunk(c), :].reshape(L * CH, 4 * C) for b in range(3)]
        return jnp.concatenate(parts, axis=1)

    def conv(lhs, kernel):
        out = jnp.dot(lhs, kernel[...], preferred_element_type=F32)
        pre[...] = out.reshape(L, CH, W)

    def kernel_grad(lhs, grad, acc):
        acc[...] += lax.dot_general(
            lhs, grad, (((0,), (0,)), ((), ())), preferred_element_type=F32
        )

    def columns(body, carry):
        return lax.fori_loop(0, L, body, carry)

    zero8 = jnp.zeros((8, W), F32)

    def arrive(c):
        loop(1, nlo, lambda k: f_copy(c, k).wait_recv())
        halo_send(X, 0, c)

    def first_chunk(c, stats):
        halo_wait(X, 0, c)
        conv(taps(X, c), w1)

        def one(j, carry):
            s, m = carry
            value, grad = smooth(pre[j])
            act[j, chunk(c), :] = value
            slope[j, chunk(c), :] = grad
            here = cnt[j, chunk(c), :]
            return s + to_eight(here * value), m + to_eight(here)

        s8, n8 = columns(one, (zero8, zero8))
        s_c, n_c = fold(total_row(s8)), fold(total_row(n8))
        mean_c = s_c / jnp.maximum(n_c, 1.0)
        mean_w = twice(mean_c)

        def two(j, m2):
            off = act[j, chunk(c), :] - mean_w
            return m2 + to_eight(cnt[j, chunk(c), :] * off * off)

        m_c = fold(total_row(columns(two, zero8)))
        n_0, s_0, m_0 = stats
        delta = mean_c - s_0 / jnp.maximum(n_0, 1.0)
        n_1 = n_0 + n_c
        m_1 = m_0 + m_c + delta * delta * (n_0 * n_c / jnp.maximum(n_1, 1.0))
        return n_1, s_0 + s_c, m_1

    def send_cot():
        def one(c):
            loop(1, nlo, lambda k: c_copy(c, k).start())
        loop(0, nch, one)

    arrive(0)
    zero1 = jnp.zeros((1, C), F32)

    def first_step(c, stats):
        @pl.when(c + 1 < nch)
        def _():
            arrive(c + 1)
            pl.when(c + 2 == nch)(send_cot)
        return first_chunk(c, stats)

    n_d, s_d, m_d = lax.fori_loop(0, nch, first_step, (zero1, zero1, zero1))

    def share(buf, which, value):
        buf[me] = value
        others(lambda i, j: remote(buf.at[me], buf.at[me], y_s.at[which], y_r.at[which], i, j).start())

    def shared(buf, which):
        block = remote(buf.at[pl.ds(0, n - 1)], buf.at[pl.ds(0, n - 1)], y_s.at[which], y_r.at[which], la, lo)
        block.wait_recv()
        block.wait_send()
        return buf[...]

    share(y1, 0, jnp.concatenate([n_d, s_d, m_d], axis=1))
    build_turned(t1)
    forward_kernel(SECOND)
    finish_kernel(SECOND)
    build_forward(w2)
    build_turned(t2)
    acc1[...] = jnp.zeros_like(acc1)
    acc2[...] = jnp.zeros_like(acc2)

    parts = shared(y1, 0)
    n_all, s_all, m_all = parts[:, :, :C], parts[:, :, C : 2 * C], parts[:, :, 2 * C :]
    total = jnp.sum(n_all, axis=0)
    center = jnp.sum(s_all, axis=0) / total
    apart = s_all / jnp.maximum(n_all, 1.0) - center[None]
    spread = jnp.sum(m_all + n_all * apart * apart, axis=0) / total
    inverse = lax.rsqrt(spread + EPS)
    gain, shift, bias = vec[0:1, :], vec[1:2, :], vec[2:3, :]
    center_w, inverse_w = twice(center), twice(inverse)
    gain_w, shift_w, bias_w = twice(gain), twice(shift), twice(bias)

    def hidden(c):
        def one(j, carry):
            normed = (act[j, chunk(c), :] - center_w) * inverse_w
            H[1 + j, chunk(c), pl.ds(C, W)] = (normed * gain_w + shift_w).astype(BF)
            return carry
        columns(one, 0)
        halo_send(H, 1, c)

    loop(0, nch, hidden)

    def out_copy(src, dst, ss, rs, c, k):
        m = peer(k)
        return remote(
            src.at[pl.ds(Q * m, Q), chunk(c), :],
            dst.at[:, pl.ds(pl.multiple_of(lo * S + c * CH, CH), CH), :],
            ss.at[c, k], rs.at[c, k], la, m,
        )

    def own_out(src, dst, ss, c):
        return pltpu.make_async_copy(
            src.at[pl.ds(Q * lo, Q), chunk(c), :],
            dst.at[:, pl.ds(pl.multiple_of(lo * S + c * CH, CH), CH), :],
            ss.at[c, 0],
        )

    def send_out(src, dst, ss, rs, c):
        loop(1, nlo, lambda k: out_copy(src, dst, ss, rs, c, k).start())
        own_out(src, dst, ss, c).start()

    def second_chunk(c, b8):
        halo_wait(H, 1, c)
        loop(1, nlo, lambda k: c_copy(c, k).wait_recv())
        lhs = taps(H, c)
        conv(lhs, w2)

        def one(j, carry):
            value, grad = smooth(pre[j] + bias_w)
            standard = X[1 + j, chunk(c), pl.ds(C, W)].astype(F32)
            bo[j, chunk(c), :] = (standard + value).astype(BF)
            low = (ct[j, chunk(c), :].astype(F32) * grad).astype(BF)
            G[1 + j, chunk(c), pl.ds(C, W)] = low
            return carry + to_eight(low.astype(F32))

        b8 = columns(one, b8)
        halo_send(G, 2, c)
        send_out(bo, ob, bo_s, bo_r, c)
        grad = G[1 : 1 + L, chunk(c), pl.ds(C, W)].reshape(L * CH, W)
        kernel_grad(taps(H, c), grad, acc2)
        return b8

    def back_chunk(c, carry):
        halo_wait(G, 2, c)
        conv(taps(G, c), t2)

        def one(j, carry):
            g8, s8 = carry
            value = pre[j]
            sg[j, chunk(c), :] = value
            normed = (act[j, chunk(c), :] - center_w) * inverse_w
            return g8 + to_eight(value * normed), s8 + to_eight(value)

        return columns(one, carry)

    b8 = second_chunk(0, zero8)

    def second_step(c, carry):
        b8, g8, s8 = carry
        b8 = second_chunk(c + 1, b8)
        g8, s8 = back_chunk(c, (g8, s8))
        return b8, g8, s8

    b8, g8, s8 = lax.fori_loop(0, nch - 1, second_step, (b8, zero8, zero8))
    g8, s8 = back_chunk(nch - 1, (g8, s8))
    sums = [fold(total_row(v)) for v in (g8, s8, b8)]
    share(y2, 1, jnp.concatenate(sums, axis=1))

    def lat_copy(k, i):
        return remote(rsb.at[k, i], rr.at[k, la], ra_s.at[k, i], ra_r.at[k, la], i, lo)

    def lat_wait(k, i):
        return remote(rsb.at[k, i], rr.at[k, i], ra_s.at[k, i], ra_r.at[k, i], i, lo)

    def lat_start(k, acc):
        for a in range(3):
            for b in range(3):
                top, low = (b * 4 + a) * C, (b * 4 + a + 1) * C
                kform[k, pl.ds((3 * a + b) * C, C), :] = (
                    acc[pl.ds(top, C), cols_of(0)] + acc[pl.ds(low, C), cols_of(1)]
                )

        def one(i):
            rows = kform[k, pl.ds(pl.multiple_of(i * z.wr, 8), z.wr), :]
            rsb[k, i] = rows.astype(BF)
            pl.when(i != la)(lambda: lat_copy(k, i).start())
        loop(0, nla, one)

    def lon_copy(k, m):
        return remote(lb.at[k, m], lr.at[k, lo], ro_s.at[k, m], ro_r.at[k, lo], la, m)

    def lon_wait(k, m):
        return remote(lb.at[k, m], lr.at[k, m], ro_s.at[k, m], ro_r.at[k, m], la, m)

    def lon_start(k):
        ssum[...] = jnp.zeros_like(ssum)
        ssum[0 : z.wr, :] = kform[k, pl.ds(pl.multiple_of(la * z.wr, 8), z.wr), :]

        def one(i):
            @pl.when(i != la)
            def _():
                lat_wait(k, i).wait_recv()
                ssum[0 : z.wr, :] += rr[k, i].astype(F32)
        loop(0, nla, one)
        ts[k] = ssum[...].T

        def two(m):
            lb[k, m] = ts[k, pl.ds(pl.multiple_of(m * z.wc, z.wc), z.wc), :].astype(BF)
            pl.when(m != lo)(lambda: lon_copy(k, m).start())
        loop(0, nlo, two)

    def lon_finish(k):
        gw[k] = ts[k, pl.ds(pl.multiple_of(lo * z.wc, z.wc), z.wc), :]

        def one(m):
            @pl.when(m != lo)
            def _():
                lon_wait(k, m).wait_recv()
                gw[k] += lr[k, m].astype(F32)
        loop(0, nlo, one)

    lat_start(SECOND, acc2)

    sums = jnp.sum(shared(y2, 1), axis=0)
    gain_grad, shift_grad = sums[:, :C], sums[:, C : 2 * C]
    gv[...] = sums

    scale_w = twice(inverse * gain)
    shift_part = twice(shift_grad / total)
    gain_part = twice(gain_grad / total)

    def first_grad(c):
        def one(j, carry):
            normed = (act[j, chunk(c), :] - center_w) * inverse_w
            here = cnt[j, chunk(c), :]
            value = sg[j, chunk(c), :] - here * shift_part - here * normed * gain_part
            low = (scale_w * value * slope[j, chunk(c), :]).astype(BF)
            F[1 + j, chunk(c), pl.ds(C, W)] = low
            return carry
        columns(one, 0)
        halo_send(F, 3, c)

    def first_kernel(c):
        grad = F[1 : 1 + L, chunk(c), pl.ds(C, W)].reshape(L * CH, W)
        kernel_grad(taps(X, c), grad, acc1)

    def field_chunk(c):
        halo_wait(F, 3, c)
        out = jnp.dot(taps(F, c), t1[...], preferred_element_type=F32)
        fs[:, chunk(c), :] = out.astype(BF).reshape(L, CH, W)
        send_out(fs, fo, fo_s, fo_r, c)

    loop(0, nch, first_grad)
    loop(0, nch, first_kernel)
    lat_start(FIRST, acc1)
    loop(0, nch, field_chunk)
    lon_start(SECOND)
    lon_start(FIRST)
    lon_finish(SECOND)
    lon_finish(FIRST)
    square = gw[0] * gw[0] + gw[1] * gw[1]
    square = total_row(square)
    share(y3, 2, sum(square[:, cols_of(t)] for t in range(z.LP // C)))
    squares = jnp.sum(shared(y3, 2), axis=0)
    mine2 = total_row((sums * sums).reshape(3, C)) if False else sum(
        sums[:, cols_of(t)] * sums[:, cols_of(t)] for t in range(3)
    )
    norm = jnp.sqrt(jnp.sum(squares + mine2, axis=1, keepdims=True))
    gn[...] = jnp.broadcast_to(norm, (1, C))

    def drain(c):
        def one(k):
            f_copy(c, k).wait_send()
            c_copy(c, k).wait_send()
            out_copy(bo, ob, bo_s, bo_r, c, k).wait()
            out_copy(fs, fo, fo_s, fo_r, c, k).wait()
        loop(1, nlo, one)
        own_out(bo, ob, bo_s, c).wait()
        own_out(fs, fo, fo_s, c).wait()
        for h, ref in enumerate((X, H, G, F)):
            halo_done(ref, h, c)

    loop(0, nch, drain)

    def drain_lon(k):
        w_copy(k).wait_send()
        mask_copy(k).wait_send()
    loop(1, nlo, drain_lon)
    for k in range(2):
        loop(1, nla // 2, lambda d: kz_copy(k, d).wait_send())
        loop(0, nla // 2, lambda d: kc_copy(k, d).wait_send())
        loop(0, nla, lambda i: pl.when(i != la)(lambda: lat_copy(k, i).wait_send()))
        loop(0, nlo, lambda m: pl.when(m != lo)(lambda: lon_copy(k, m).wait_send()))


def adam_step(master, first, second, grads, rate, decay):
    first_new = BETA_ONE * first + (1.0 - BETA_ONE) * grads
    second_new = BETA_TWO * second + (1.0 - BETA_TWO) * grads * grads
    first_hat = first_new / (1.0 - BETA_ONE**STEP)
    second_hat = second_new / (1.0 - BETA_TWO**STEP)
    master_new = master - rate * (first_hat / (jnp.sqrt(second_hat) + ADAM_EPS) + decay * master)
    return master_new, first_new, second_new


def last_kernel(
    z, step,
    ob, fo, cot, missing, std, gw, gv, gn, wm, wf, wsec, vm, vf, vs,
    block_out, field_grad, norm, w_new, w_first, w_second, w_low, v_new, v_first, v_second,
    cf, bf,
):
    Q = z.Q
    present, _ = both_masks(missing[...], None)
    have = present.T
    rstd = 1.0 / std[...]
    cf[...] = cot[...].astype(F32)
    for p in range(z.PX):
        i, q = p // Q, p % Q
        here = pl.ds(p, step, stride=z.PX)
        grad = cf[here, :] + fo[q, :, cols_of(i)].astype(F32)
        field_grad[here, :] = grad * have[:, p : p + 1] * rstd
        bf[here, :] = ob[q, :, cols_of(i)].astype(F32)
    block_out[...] = bf[...].astype(BF)

    @pl.when(pl.program_id(0) == 0)
    def _():
        size = gn[...]
        norm[...] = size[:, 0:1]
        factor = jnp.minimum(1.0, MAX_NORM / size)
        wide = factor[:, 0:1]
        for k in range(2):
            grads = gw[k, :, 0 : z.wr] * wide
            new, first, second = adam_step(wm[k], wf[k], wsec[k], grads, RATE_KERNEL, DECAY)
            w_new[k], w_first[k], w_second[k] = new, first, second
            w_low[k] = new.astype(BF)
        for k in range(3):
            grads = gv[:, cols_of(k)] * factor
            row = slice(k, k + 1)
            new, first, second = adam_step(vm[row, :], vf[row, :], vs[row, :], grads, RATE_VECTOR, 0.0)
            v_new[row, :], v_first[row, :], v_second[row, :] = new, first, second


def body(nla, nlo, fields, chan_mean, chan_std, sea_mask, missing, cotangent,
         w_master, w_first, w_second, vec_master, vec_first, vec_second):
    samples, rows, quads, channels = fields.shape
    z = Sizes(nla, nlo, samples, quads, w_master.shape[1], w_master.shape[2])
    S, L, Q, CH, nch, n, B = z.S, z.L, z.Q, z.CH, z.nch, z.n, z.B
    flat = (samples * rows * quads, channels)
    fields = fields.reshape(flat)
    cotangent = cotangent.reshape(flat)
    sea = jnp.transpose(sea_mask, (1, 2, 0))
    miss = jnp.transpose(missing, (1, 2, 0))
    wm, wf, wsec = (jnp.transpose(w, (0, 2, 1)) for w in (w_master, w_first, w_second))
    mean, std = chan_mean.reshape(1, C), chan_std.reshape(1, C)

    vmem = pl.BlockSpec(memory_space=pltpu.VMEM)
    hbm = pl.BlockSpec(memory_space=pl.ANY)
    V = pltpu.VMEM
    dma = pltpu.SemaphoreType.DMA
    shape = jax.ShapeDtypeStruct
    padded = V((L + 2, S, 4 * C), BF)
    wide = V((L, S, W), F32)
    scratch = [
        V(flat, BF), V(flat, BF), V((CH * z.PX, C), F32), V((B, z.PX), F32),
        V((nlo, z.PX, B), F32), wide,
        V((nch, nlo, Q, CH, W), BF), V((nch, nlo, Q, CH, W), BF),
        padded, padded, padded, padded, wide, wide, wide,
        V((L, S, W), BF), V((L, CH, W), F32), V((L, S, W), BF), V((L, S, W), BF),
        V((12 * C, W), BF), V((12 * C, W), BF), V((12 * C, W), BF), V((12 * C, W), BF),
        V((12 * C, W), F32), V((12 * C, W), F32),
        V((2, z.wc, z.LP), BF), V((nlo, 2, z.wc, z.LP), BF), V((2, nla, z.wr, C), BF),
        V((9 * C, C), F32), V((2, z.wr, C), BF),
        V((2, nla, z.wr, C), BF), V((2, nla, z.wr, C), BF), V((2, 9 * C, C), F32),
        V((z.LP, C), F32), V((2, C, z.LP), F32), V((2, nlo, z.wc, z.LP), BF), V((2, nlo, z.wc, z.LP), BF),
        V((n, 1, 3 * C), F32), V((n, 1, 3 * C), F32), V((n, 1, C), F32),
        dma((2,)), dma((nlo,)), dma((nlo,)), dma((nch, nlo)), dma((nch, nlo)),
        dma((nch, nlo)), dma((nch, nlo)), dma((4, nch, 2)), dma((4, nch, 2)),
        dma((nch, nlo)), dma((nch, nlo)), dma((nch, nlo)), dma((nch, nlo)),
        dma((nlo,)), dma((nlo,)), dma((2, nla)), dma((2, nla)), dma((2, nla)), dma((2, nla)),
        dma((2, nla)), dma((2, nla)), dma((2, nlo)), dma((2, nlo)), dma((3,)), dma((3,)),
    ]
    ob, fo, gw, gv, gn = pl.pallas_call(
        functools.partial(main_kernel, z),
        out_shape=(
            shape((Q, B, W), BF), shape((Q, B, W), BF),
            shape((2, z.wc, z.LP), F32), shape((1, 3 * C), F32), shape((1, C), F32),
        ),
        in_specs=[hbm, hbm] + [vmem] * 6,
        out_specs=(hbm, hbm, vmem, vmem, vmem),
        scratch_shapes=scratch,
        compiler_params=pltpu.CompilerParams(
            collective_id=0, has_side_effects=True, vmem_limit_bytes=56 * 2**20
        ),
        name="block",
    )(fields, cotangent, sea, miss, mean, std, wm, vec_master)

    step = min(128, B)
    whole = lambda s: pl.BlockSpec(s, lambda t: (0,) * len(s))
    native = pl.BlockSpec((step * z.PX, C), lambda t: (t, 0))
    spread = pl.BlockSpec((Q, step, W), lambda t: (0, t, 0))
    w_spec, v_spec = whole(wm.shape), whole((3, C))
    outs = pl.pallas_call(
        functools.partial(last_kernel, z, step),
        grid=(B // step,),
        out_shape=(
            shape(flat, BF), shape(flat, F32), shape((1, 1), F32),
            shape(wm.shape, F32), shape(wm.shape, F32), shape(wm.shape, F32), shape(wm.shape, BF),
            shape((3, C), F32), shape((3, C), F32), shape((3, C), F32),
        ),
        in_specs=[
            spread, spread, native, pl.BlockSpec((R, Q, step), lambda t: (0, 0, t)), whole((1, C)),
            whole(gw.shape), whole(gv.shape), whole(gn.shape),
            w_spec, w_spec, w_spec, v_spec, v_spec, v_spec,
        ],
        out_specs=(native, native, whole((1, 1)), w_spec, w_spec, w_spec, w_spec, v_spec, v_spec, v_spec),
        scratch_shapes=[V((step * z.PX, C), F32), V((step * z.PX, C), F32)],
        compiler_params=pltpu.CompilerParams(vmem_limit_bytes=32 * 2**20),
        name="update",
    )(ob, fo, cotangent, miss, std, gw, gv, gn, wm, wf, wsec, vec_master, vec_first, vec_second)
    block_out, field_grad, norm, w_new, w_f, w_s, w_low, v_new, v_f, v_s = outs
    like = (samples, rows, quads, channels)
    w_new, w_f, w_s, w_low = (jnp.transpose(w, (0, 2, 1)) for w in (w_new, w_f, w_s, w_low))
    return (
        block_out.reshape(like), field_grad.reshape(like), norm.reshape(()),
        w_new, w_f, w_s, w_low, v_new, v_f, v_s,
    )


def solution(mesh):
    tile, kernel = P(None, "lat", "lon", None), P(None, "lat", "lon")
    return jax.shard_map(
        functools.partial(body, mesh.shape["lat"], mesh.shape["lon"]),
        mesh=mesh,
        in_specs=(tile, P(), P(), kernel, kernel, tile, kernel, kernel, kernel, P(), P(), P()),
        out_specs=(tile, tile, P(), kernel, kernel, kernel, kernel, P(), P(), P()),
        check_vma=False,
    )
```

profile of v0, /device:TPU:0, one launch (start us, length us, event | category | flops | bytes accessed | tf_op | source)
XLA Modules:
  0.0 107.5 jit_solution(11336448314934119011)
XLA Ops:
  0.6 0.0 copy-start.8
  0.7 0.0 copy-start.11
  0.7 0.0 copy-start.10
  0.7 0.0 copy-start.6
  0.7 0.0 copy-start.5
  0.7 0.0 copy-start.3
  0.7 0.0 copy-start
  0.7 0.0 copy-start.4
  0.7 0.0 copy-start.9
  0.7 98.7 %block.1 = (bf16[4,512,256]{2,1,0:T(8,128)(2,1)}, bf16[4,512,256]{2,1,0:T(8,128)(2,1)}, f32[2,32,256]{2,1,0:T(8,128)}, f32[1,384]{1,0:T(1,128)}, f32[1,128]{1,0:T(1,128)}) custom-call(bf16[4096,128]{1,0:T(8,128)(2,1)} %bitcast.26, bf16[4096,128]{1,0:T(8,128)(2,1)} %bitcast.16, s32[2,4,512]{2,1,0:T(4,128)} %bitcast.27, s32[2,4,512]{2,1,0:T(4,128)} %bitcast.20, ...), custom_call_target="tpu_custom_call" | custom-call | tf_op jit(solution)/shard_map/block/pallas_call | solution.py:704
  99.5 0.0 copy-done.8
  99.5 0.0 copy-done.11
  99.5 0.0 copy-done.10
  99.5 0.0 copy-done.6
  99.5 0.0 copy-done.5
  99.5 0.0 copy-done.3
  99.5 0.0 copy-done
  99.5 0.0 copy-done.4
  99.6 0.0 copy-done.9
  99.6 0.0 copy-start.1
  99.6 1.2 %copy-done.1 = bf16[4,512,256]{2,1,0:T(8,128)(2,1)S(1)} copy-done((bf16[4,512,256]{2,1,0:T(8,128)(2,1)S(1)}, bf16[4,512,256]{2,1,0:T(8,128)(2,1)}, u32[]{:S(2)}) %copy-start.1) | copy-done | bytes 1048600
  100.8 0.0 copy-start.2
  100.8 1.2 %copy-done.2 = bf16[4,512,256]{2,1,0:T(8,128)(2,1)S(1)} copy-done((bf16[4,512,256]{2,1,0:T(8,128)(2,1)S(1)}, bf16[4,512,256]{2,1,0:T(8,128)(2,1)}, u32[]{:S(2)}) %copy-start.2) | copy-done | bytes 1048600
  102.0 0.0 copy-start.7
  102.0 0.8 copy-done.7
  102.9 0.0 copy-start.12
  102.9 0.7 copy-done.12
  103.5 0.0 copy-start.13
  103.5 0.6 copy-done.13
  104.1 3.4 %update.1 = (bf16[4096,128]{1,0:T(8,128)(2,1)}, f32[4096,128]{1,0:T(8,128)}, f32[1,1]{1,0:T(1,128)}, f32[2,32,144]{2,1,0:T(8,128)}, f32[2,32,144]{2,1,0:T(8,128)...) custom-call(bf16[4,512,256]{2,1,0:T(8,128)(2,1)S(1)} %copy-done.1, ...), custom_call_target="tpu_custom_call" | custom-call | tf_op jit(solution)/shard_map/update/pallas_call | solution.py:724
Async XLA Ops:
  0.6 98.8 %copy-start.8 = (f32[3,128]{1,0:T(4,128)S(1)}, f32[3,128]{1,0:T(4,128)}, u32[]{:S(2)}) copy-start(f32[3,128]{1,0:T(4,128)} %vm.1) | copy-start | bytes 4612
  0.7 98.8 %copy-start.11 = (f32[3,128]{1,0:T(4,128)S(1)}, f32[3,128]{1,0:T(4,128)}, u32[]{:S(2)}) copy-start(f32[3,128]{1,0:T(4,128)} %vs.1) | copy-start | bytes 4612
  0.7 98.8 %copy-start.10 = (f32[3,128]{1,0:T(4,128)S(1)}, f32[3,128]{1,0:T(4,128)}, u32[]{:S(2)}) copy-start(f32[3,128]{1,0:T(4,128)} %vf.1) | copy-start | bytes 4612
  0.7 98.8 %copy-start.6 = (f32[2,144,32]{1,2,0:T(8,128)S(1)}, f32[2,144,32]{1,2,0:T(8,128)}, u32[]{:S(2)}) copy-start(f32[2,144,32]{1,2,0:T(8,128)} %param.20) | copy-start | bytes 110596
  0.7 98.8 %copy-start.5 = (f32[2,144,32]{1,2,0:T(8,128)S(1)}, f32[2,144,32]{1,2,0:T(8,128)}, u32[]{:S(2)}) copy-start(f32[2,144,32]{1,2,0:T(8,128)} %param.19) | copy-start | bytes 110596
  0.7 98.8 %copy-start.3 = (f32[2,144,32]{1,2,0:T(8,128)S(1)}, f32[2,144,32]{1,2,0:T(8,128)}, u32[]{:S(2)}) copy-start(f32[2,144,32]{1,2,0:T(8,128)} %param.18) | copy-start | bytes 110596
  0.7 98.8 %copy-start = (bf16[512,2,4,128]{3,2,1,0:T(4,128)(2,1)S(1)}, bf16[512,2,4,128]{3,2,1,0:T(4,128)(2,1)}, u32[]{:S(2)}) copy-start(bf16[512,2,4,128]{3,2,1,0:T(4,128)(2,1)} %param.17) | copy-start | bytes 3145732
  0.7 98.8 %copy-start.4 = (s32[512,2,4]{0,2,1:T(4,128)S(1)}, s32[512,2,4]{0,2,1:T(4,128)}, u32[]{:S(2)}) copy-start(s32[512,2,4]{0,2,1:T(4,128)} %param.16) | copy-start | bytes 49156
  0.7 98.8 %copy-start.9 = (f32[128]{0:T(128)S(1)}, f32[128]{0:T(128)}, u32[]{:S(2)}) copy-start(f32[128]{0:T(128)} %param.14) | copy-start | bytes 1540
  99.6 1.2 %copy-start.1 = (bf16[4,512,256]{2,1,0:T(8,128)(2,1)S(1)}, bf16[4,512,256]{2,1,0:T(8,128)(2,1)}, u32[]{:S(2)}) copy-start(bf16[4,512,256]{2,1,0:T(8,128)(2,1)} %get-tuple-element.25.ob) | copy-start | bytes 3145732
  100.8 1.2 %copy-start.2 = (bf16[4,512,256]{2,1,0:T(8,128)(2,1)S(1)}, bf16[4,512,256]{2,1,0:T(8,128)(2,1)}, u32[]{:S(2)}) copy-start(bf16[4,512,256]{2,1,0:T(8,128)(2,1)} %get-tuple-element.26.fo) | copy-start | bytes 3145732
  102.0 0.8 copy-start.7
  102.9 0.7 copy-start.12
  103.5 0.6 copy-start.13
where the time goes:
time: 108 us
  Pallas kernels  102 us (94%)
  local copies, waits for them, and re-layouts  4.58 us (4%)
    pallas_call x1, Pallas kernels, body(): pl.pallas_call(functools.partial(main_kernel, z), out_shape=(shape((Q, B,...  98.7 us
    unnamed x28, local copies, waits for them, and re-layouts  4.58 us
    pallas_call x1, Pallas kernels, body(): pl.pallas_call(functools.partial(last_kernel, z, step), grid=(B // step,)...  3.38 us

commit v1 on v0

--- a/solution.py
+++ b/solution.py
@@ -81,17 +81,17 @@
 
 def main_kernel(
     z,
-    fields, cot, sea, missing, mean, std, wt, vec,
-    ob, fo, gw, gv, gn,
-    fin, cin, fb, pres, cm, cnt, sb, cb,
+    fields, cot, sea_h, missing_h, mean_h, std_h, wt_h, vec_h,
+    ob, fo, grads,
+    fin, cin, sea, missing, mean, std, wt, vec, fb, pres, cm, cnt, sb, cb,
     X, H, G, F, act, slope, sg, ct, pre, bo, fs,
     w1, w2, t1, t2, acc1, acc2,
     ws, wg, kg_in, kf, kl,
-    rsb, rr, kform, ssum, ts, lb, lr,
+    ca, cr, za, zr, kform, ssum, ts, lb, lr,
     y1, y2, y3,
     load_sem, mask_s, mask_r, f_s, f_r, c_s, c_r, halo_s, halo_r,
-    bo_s, bo_r, fo_s, fo_r, wg_s, wg_r, kz_s, kz_r, kc_s, kc_r,
-    ra_s, ra_r, ro_s, ro_r, y_s, y_r,
+    bo_s, bo_r, bo_o, fo_s, fo_r, fo_o, wg_s, wg_r, kz_s, kz_r, kc_s, kc_r,
+    rc_s, rc_r, rz_s, rz_r, ro_s, ro_r, y_s, y_r,
 ):
     nla, nlo, n = z.nla, z.nlo, z.n
     S, L, Q, CH, nch = z.S, z.L, z.Q, z.CH, z.nch
@@ -104,6 +104,12 @@
             src, dst, ss, rs, device_id=(lat_to, lon_to), device_id_type=MESH
         )
 
+    def received(ref, sem):
+        remote(ref, ref, sem, sem, la, lo).wait_recv()
+
+    def sent(ref, sem):
+        remote(ref, ref, sem, sem, la, lo).wait_send()
+
     def loop(low, high, body):
         def step(k, carry):
             body(k)
@@ -111,7 +117,11 @@
         lax.fori_loop(low, high, step, 0)
 
     def others(body):
-        def row(i):
+        upper = la // (nla // 2)
+
+        def row(t):
+            i = upper * t + (1 - upper) * (nla - 1 - t)
+
             def one(j):
                 @pl.when(jnp.logical_or(i != la, j != lo))
                 def _():
@@ -119,6 +129,8 @@
             loop(0, nlo, one)
         loop(0, nla, row)
 
+    own = pl.ds(C, W)
+
     def chunk(c):
         return pl.ds(pl.multiple_of(c * CH, CH), CH)
 
@@ -127,10 +139,16 @@
 
     barrier = pltpu.get_barrier_semaphore()
     others(lambda i, j: pl.semaphore_signal(barrier, inc=1, device_id=(i, j), device_id_type=MESH))
-    load_f = pltpu.make_async_copy(fields, fin, load_sem.at[0])
-    load_c = pltpu.make_async_copy(cot, cin, load_sem.at[1])
-    load_f.start()
-    load_c.start()
+    pairs = (
+        (missing_h, missing), (sea_h, sea), (mean_h, mean), (std_h, std), (wt_h, wt), (vec_h, vec),
+        (fields, fin), (cot, cin),
+    )
+    loads = [pltpu.make_async_copy(src, dst, load_sem.at[i]) for i, (src, dst) in enumerate(pairs)]
+    for load in loads:
+        load.start()
+    for load in loads[:-2]:
+        load.wait()
+    load_f, load_c = loads[-2:]
 
     present, counted = both_masks(missing[...], sea[...])
     pres[...] = present.T
@@ -142,25 +160,23 @@
             block = jnp.concatenate([block, jnp.zeros((z.wc, pad), BF)], axis=1)
         ws[k] = block
         wg[lo, k] = block
+    north_pole, south_pole = la == 0, la == nla - 1
     for ref in (X, H, G, F):
-        @pl.when(la == 0)
+        @pl.when(north_pole)
         def _():
             ref[:, :, cols_of(0)] = jnp.zeros((L + 2, S, C), BF)
 
-        @pl.when(la == nla - 1)
+        @pl.when(south_pole)
         def _():
             ref[:, :, cols_of(3)] = jnp.zeros((L + 2, S, C), BF)
 
-    pl.semaphore_wait(barrier, n - 1)
-
     def w_copy(k):
         m = peer(k)
-        return remote(ws, wg.at[lo], wg_s.at[k], wg_r.at[k], la, m)
+        return remote(ws, wg.at[lo], wg_s.at[0], wg_r.at[0], la, m)
 
     def mask_copy(k):
-        return remote(cm.at[lo], cm.at[lo], mask_s.at[k], mask_r.at[k], la, peer(k))
-
-    loop(1, nlo, lambda k: w_copy(k).start())
+        return remote(cm.at[lo], cm.at[lo], mask_s.at[0], mask_r.at[0], la, peer(k))
+
     load_f.wait()
 
     rstd = 1.0 / std[...]
@@ -178,23 +194,29 @@
 
     def f_copy(c, k):
         return remote(
-            sb.at[c, k], X.at[pl.ds(1 + Q * lo, Q), chunk(c), pl.ds(C, W)],
-            f_s.at[c, k], f_r.at[c, k], la, peer(k),
+            sb.at[c, k], X.at[pl.ds(1 + Q * lo, Q), chunk(c), own],
+            f_s.at[0], f_r.at[c], la, peer(k),
         )
 
     def c_copy(c, k):
         return remote(
             cb.at[c, k], ct.at[pl.ds(Q * lo, Q), chunk(c), :],
-            c_s.at[c, k], c_r.at[c, k], la, peer(k),
+            c_s.at[0], c_r.at[c], la, peer(k),
         )
 
-    def send_fields(c):
+    def prep_fields(c):
         def one(k):
             def put(i, q, value):
                 sb[c, k, q, :, cols_of(i)] = value
             place(fin, peer(k), c, put, True)
-            f_copy(c, k).start()
         loop(1, nlo, one)
+
+    def send_fields(c):
+        loop(1, nlo, lambda k: f_copy(c, k).start())
+
+    def next_fields(c):
+        prep_fields(c)
+        send_fields(c)
 
     def own_fields(c):
         def put(i, q, value):
@@ -213,11 +235,14 @@
             place(cin, peer(k), c, put, False)
         loop(1, nlo, one)
 
-    loop(0, nch, send_fields)
+    prep_fields(0)
+    pl.semaphore_wait(barrier, n - 1)
+    loop(1, nlo, lambda k: w_copy(k).start())
     loop(1, nlo, lambda k: mask_copy(k).start())
-    loop(0, nch, own_fields)
-
-    loop(1, nlo, lambda k: w_copy(k).wait_recv())
+    send_fields(0)
+    loop(1, nch, next_fields)
+
+    received(wg.at[pl.ds(0, nlo - 1)], wg_r.at[0])
     for k in range(2):
         gathered = jnp.concatenate([wg[m, k].astype(F32) for m in range(nlo)], axis=0)
         kl[k] = gathered.T[: z.wr].astype(BF)
@@ -227,24 +252,22 @@
 
     def kz_copy(k, d):
         to = lax.rem(la + 2 * d, nla)
-        return remote(kl.at[k], kg_in.at[k, la], kz_s.at[k, d], kz_r.at[k, d], to, lo)
+        return remote(kl.at[k], kg_in.at[k, la], kz_s.at[k], kz_r.at[k], to, lo)
 
     def kc_copy(k, d):
         row = lax.rem(la + nla - 2 * d, nla)
-        return remote(kg_in.at[k, row], kg_in.at[k, row], kc_s.at[k, d], kc_r.at[k, d], sibling, lo)
+        return remote(kg_in.at[k, row], kg_in.at[k, row], kc_s.at[k], kc_r.at[k], sibling, lo)
 
     def start_kernel(k):
         loop(1, nla // 2, lambda d: kz_copy(k, d).start())
         kc_copy(k, 0).start()
 
     def forward_kernel(k):
-        def one(d):
-            kz_copy(k, d).wait_recv()
-            kc_copy(k, d).start()
-        loop(1, nla // 2, one)
+        received(kg_in.at[k, pl.ds(0, nla // 2 - 1)], kz_r.at[k])
+        loop(1, nla // 2, lambda d: kc_copy(k, d).start())
 
     def finish_kernel(k):
-        loop(0, nla // 2, lambda d: kc_copy(k, d).wait_recv())
+        received(kg_in.at[k, pl.ds(0, nla // 2)], kc_r.at[k])
         for i in range(nla):
             kf[pl.ds(i * z.wr, z.wr), :] = kg_in[k, i].astype(F32)
 
@@ -272,31 +295,26 @@
     start_kernel(FIRST)
     start_kernel(SECOND)
 
+    loop(0, nch, own_fields)
     load_c.wait()
     loop(0, nch, own_cot)
     loop(0, nch, prep_cot)
-    loop(1, nlo, lambda k: mask_copy(k).wait_recv())
-    rows = jnp.concatenate([cm[m] for m in range(nlo)], axis=0)
-    back = z.B - lo * S
-    mine = pltpu.roll(rows, lax.rem(back, z.B), 1)[:, : min(z.B, 128)].T
-    for j in range(L):
-        for i in range(R):
-            col = (j // Q) * z.PX + i * Q + j % Q
-            cnt[j, :, cols_of(i)] = jnp.broadcast_to(mine[:S, col : col + 1], (S, C))
-
-    forward_kernel(FIRST)
-    finish_kernel(FIRST)
-    build_forward(w1)
+
+    def spread_mask():
+        rows = jnp.concatenate([cm[m] for m in range(nlo)], axis=0)
+        back = z.B - lo * S
+        mine = pltpu.roll(rows, lax.rem(back, z.B), 1)[:, : min(z.B, 128)].T
+        for j in range(L):
+            for i in range(R):
+                col = (j // Q) * z.PX + i * Q + j % Q
+                cnt[j, :, cols_of(i)] = jnp.broadcast_to(mine[:S, col : col + 1], (S, C))
 
     def halo_copies(ref, h, c):
-        north = remote(
-            ref.at[pl.ds(1, L), chunk(c), pl.ds(C, C)], ref.at[pl.ds(1, L), chunk(c), pl.ds(3 * C, C)],
-            halo_s.at[h, c, 0], halo_r.at[h, c, 0], jnp.maximum(la - 1, 0), lo,
-        )
-        south = remote(
-            ref.at[pl.ds(1, L), chunk(c), pl.ds(2 * C, C)], ref.at[pl.ds(1, L), chunk(c), pl.ds(0, C)],
-            halo_s.at[h, c, 1], halo_r.at[h, c, 1], jnp.minimum(la + 1, nla - 1), lo,
-        )
+        def lanes(r):
+            return ref.at[pl.ds(1, L), chunk(c), pl.ds(r * C, C)]
+
+        north = remote(lanes(1), lanes(3), halo_s.at[h], halo_r.at[h, c], jnp.maximum(la - 1, 0), lo)
+        south = remote(lanes(2), lanes(0), halo_s.at[h], halo_r.at[h, c], jnp.minimum(la + 1, nla - 1), lo)
         return north, south
 
     def halo_send(ref, h, c):
@@ -304,17 +322,21 @@
         pl.when(la > 0)(north.start)
         pl.when(la < nla - 1)(south.start)
 
+    at_pole = jnp.logical_or(north_pole, south_pole)
+
     def halo_wait(ref, h, c):
-        north, south = halo_copies(ref, h, c)
-        pl.when(la < nla - 1)(north.wait_recv)
-        pl.when(la > 0)(south.wait_recv)
+        def both(width):
+            received(ref.at[pl.ds(1, L), chunk(c), pl.ds(0, width)], halo_r.at[h, c])
+        pl.when(at_pole)(lambda: both(C))
+        pl.when(jnp.logical_not(at_pole))(lambda: both(W))
         ref[0, chunk(c), :] = ref[L, chunk(c), :]
         ref[L + 1, chunk(c), :] = ref[1, chunk(c), :]
 
-    def halo_done(ref, h, c):
-        north, south = halo_copies(ref, h, c)
-        pl.when(la > 0)(north.wait_send)
-        pl.when(la < nla - 1)(south.wait_send)
+    def halo_done(ref, h):
+        def both(width):
+            sent(ref.at[pl.ds(1, L), :, pl.ds(0, width)], halo_s.at[h])
+        pl.when(at_pole)(lambda: both(C))
+        pl.when(jnp.logical_not(at_pole))(lambda: both(W))
 
     def taps(ref, c):
         parts = [ref[b : b + L, chunk(c), :].reshape(L * CH, 4 * C) for b in range(3)]
@@ -330,12 +352,12 @@
         )
 
     def columns(body, carry):
-        return lax.fori_loop(0, L, body, carry)
+        return lax.fori_loop(0, L, body, carry, unroll=min(L, 16))
 
     zero8 = jnp.zeros((8, W), F32)
 
     def arrive(c):
-        loop(1, nlo, lambda k: f_copy(c, k).wait_recv())
+        received(X.at[pl.ds(1, Q * (nlo - 1)), chunk(c), own], f_r.at[c])
         halo_send(X, 0, c)
 
     def first_chunk(c, stats):
@@ -366,19 +388,21 @@
         m_1 = m_0 + m_c + delta * delta * (n_0 * n_c / jnp.maximum(n_1, 1.0))
         return n_1, s_0 + s_c, m_1
 
-    def send_cot():
-        def one(c):
-            loop(1, nlo, lambda k: c_copy(c, k).start())
-        loop(0, nch, one)
+    def send_cot(c):
+        loop(1, nlo, lambda k: c_copy(c, k).start())
 
     arrive(0)
+    forward_kernel(FIRST)
+    received(cm.at[pl.ds(0, nlo - 1)], mask_r.at[0])
+    spread_mask()
+    finish_kernel(FIRST)
+    build_forward(w1)
+    build_turned(t1)
     zero1 = jnp.zeros((1, C), F32)
 
     def first_step(c, stats):
-        @pl.when(c + 1 < nch)
-        def _():
-            arrive(c + 1)
-            pl.when(c + 2 == nch)(send_cot)
+        pl.when(c + 1 < nch)(lambda: arrive(c + 1))
+        pl.when(c + 2 == nch)(lambda: send_cot(0))
         return first_chunk(c, stats)
 
     n_d, s_d, m_d = lax.fori_loop(0, nch, first_step, (zero1, zero1, zero1))
@@ -394,7 +418,7 @@
         return buf[...]
 
     share(y1, 0, jnp.concatenate([n_d, s_d, m_d], axis=1))
-    build_turned(t1)
+    loop(1, nch, send_cot)
     forward_kernel(SECOND)
     finish_kernel(SECOND)
     build_forward(w2)
@@ -416,52 +440,59 @@
     def hidden(c):
         def one(j, carry):
             normed = (act[j, chunk(c), :] - center_w) * inverse_w
-            H[1 + j, chunk(c), pl.ds(C, W)] = (normed * gain_w + shift_w).astype(BF)
+            H[1 + j, chunk(c), own] = (normed * gain_w + shift_w).astype(BF)
             return carry
         columns(one, 0)
         halo_send(H, 1, c)
-
-    loop(0, nch, hidden)
 
     def out_copy(src, dst, ss, rs, c, k):
         m = peer(k)
         return remote(
             src.at[pl.ds(Q * m, Q), chunk(c), :],
             dst.at[:, pl.ds(pl.multiple_of(lo * S + c * CH, CH), CH), :],
-            ss.at[c, k], rs.at[c, k], la, m,
+            ss.at[0], rs.at[0], la, m,
         )
 
-    def own_out(src, dst, ss, c):
+    def own_out(src, dst, os, c):
         return pltpu.make_async_copy(
             src.at[pl.ds(Q * lo, Q), chunk(c), :],
             dst.at[:, pl.ds(pl.multiple_of(lo * S + c * CH, CH), CH), :],
-            ss.at[c, 0],
+            os.at[0],
         )
 
-    def send_out(src, dst, ss, rs, c):
+    def send_out(src, dst, ss, rs, os, c):
         loop(1, nlo, lambda k: out_copy(src, dst, ss, rs, c, k).start())
-        own_out(src, dst, ss, c).start()
+        own_out(src, dst, os, c).start()
+
+    def out_done(src, dst, ss, rs, os):
+        sent(src.at[pl.ds(0, Q * (nlo - 1))], ss.at[0])
+        received(dst.at[:, pl.ds(0, S * (nlo - 1)), :], rs.at[0])
+        pltpu.make_async_copy(src.at[pl.ds(0, Q)], dst.at[:, pl.ds(0, S), :], os.at[0]).wait()
+
+    block_out = (bo, ob, bo_s, bo_r, bo_o)
+    field_out = (fs, fo, fo_s, fo_r, fo_o)
+    early = min(1, nch - 1)
 
     def second_chunk(c, b8):
         halo_wait(H, 1, c)
-        loop(1, nlo, lambda k: c_copy(c, k).wait_recv())
-        lhs = taps(H, c)
-        conv(lhs, w2)
+        received(ct.at[pl.ds(0, Q * (nlo - 1)), chunk(c), :], c_r.at[c])
+        conv(taps(H, c), w2)
 
         def one(j, carry):
             value, grad = smooth(pre[j] + bias_w)
-            standard = X[1 + j, chunk(c), pl.ds(C, W)].astype(F32)
+            standard = X[1 + j, chunk(c), own].astype(F32)
             bo[j, chunk(c), :] = (standard + value).astype(BF)
             low = (ct[j, chunk(c), :].astype(F32) * grad).astype(BF)
-            G[1 + j, chunk(c), pl.ds(C, W)] = low
+            G[1 + j, chunk(c), own] = low
             return carry + to_eight(low.astype(F32))
 
         b8 = columns(one, b8)
         halo_send(G, 2, c)
-        send_out(bo, ob, bo_s, bo_r, c)
-        grad = G[1 : 1 + L, chunk(c), pl.ds(C, W)].reshape(L * CH, W)
+        return b8
+
+    def second_kernel(c):
+        grad = G[1 : 1 + L, chunk(c), own].reshape(L * CH, W)
         kernel_grad(taps(H, c), grad, acc2)
-        return b8
 
     def back_chunk(c, carry):
         halo_wait(G, 2, c)
@@ -476,26 +507,33 @@
 
         return columns(one, carry)
 
+    loop(0, nch, hidden)
     b8 = second_chunk(0, zero8)
 
     def second_step(c, carry):
         b8, g8, s8 = carry
         b8 = second_chunk(c + 1, b8)
+        pl.when(c < early)(lambda: send_out(*block_out, c))
+        second_kernel(c)
         g8, s8 = back_chunk(c, (g8, s8))
         return b8, g8, s8
 
     b8, g8, s8 = lax.fori_loop(0, nch - 1, second_step, (b8, zero8, zero8))
+    second_kernel(nch - 1)
     g8, s8 = back_chunk(nch - 1, (g8, s8))
     sums = [fold(total_row(v)) for v in (g8, s8, b8)]
     share(y2, 1, jnp.concatenate(sums, axis=1))
-
-    def lat_copy(k, i):
-        return remote(rsb.at[k, i], rr.at[k, la], ra_s.at[k, i], ra_r.at[k, la], i, lo)
-
-    def lat_wait(k, i):
-        return remote(rsb.at[k, i], rr.at[k, i], ra_s.at[k, i], ra_r.at[k, i], i, lo)
-
-    def lat_start(k, acc):
+    loop(early, nch, lambda c: send_out(*block_out, c))
+
+    chip, chips = la // 2, nla // 2
+
+    def rows_of(k, i):
+        return kform[k, pl.ds(pl.multiple_of(i * z.wr, 8), z.wr), :]
+
+    def core_copy(k):
+        return remote(ca.at[k], cr.at[k], rc_s.at[k], rc_r.at[k], sibling, lo)
+
+    def core_start(k, acc):
         for a in range(3):
             for b in range(3):
                 top, low = (b * 4 + a) * C, (b * 4 + a + 1) * C
@@ -503,29 +541,38 @@
                     acc[pl.ds(top, C), cols_of(0)] + acc[pl.ds(low, C), cols_of(1)]
                 )
 
-        def one(i):
-            rows = kform[k, pl.ds(pl.multiple_of(i * z.wr, 8), z.wr), :]
-            rsb[k, i] = rows.astype(BF)
-            pl.when(i != la)(lambda: lat_copy(k, i).start())
-        loop(0, nla, one)
+        def one(t):
+            ca[k, t] = rows_of(k, 2 * t + 1 - core).astype(BF)
+        loop(0, chips, one)
+        core_copy(k).start()
+
+    def chip_copy(k, t, slot):
+        return remote(za.at[k, t], zr.at[k, slot], rz_s.at[k], rz_r.at[k], 2 * t + core, lo)
+
+    def chip_start(k):
+        core_copy(k).wait_recv()
+        ssum[k] = jnp.zeros_like(ssum[k])
+        ssum[k, 0 : z.wr, :] = rows_of(k, la) + cr[k, chip].astype(F32)
+
+        def one(t):
+            @pl.when(t != chip)
+            def _():
+                za[k, t] = (rows_of(k, 2 * t + core) + cr[k, t].astype(F32)).astype(BF)
+                chip_copy(k, t, chip).start()
+        loop(0, chips, one)
 
     def lon_copy(k, m):
-        return remote(lb.at[k, m], lr.at[k, lo], ro_s.at[k, m], ro_r.at[k, lo], la, m)
-
-    def lon_wait(k, m):
-        return remote(lb.at[k, m], lr.at[k, m], ro_s.at[k, m], ro_r.at[k, m], la, m)
+        return remote(lb.at[k, m], lr.at[k, lo], ro_s.at[k], ro_r.at[k], la, m)
 
     def lon_start(k):
-        ssum[...] = jnp.zeros_like(ssum)
-        ssum[0 : z.wr, :] = kform[k, pl.ds(pl.multiple_of(la * z.wr, 8), z.wr), :]
-
-        def one(i):
-            @pl.when(i != la)
+        received(zr.at[k, pl.ds(0, chips - 1)], rz_r.at[k])
+
+        def one(t):
+            @pl.when(t != chip)
             def _():
-                lat_wait(k, i).wait_recv()
-                ssum[0 : z.wr, :] += rr[k, i].astype(F32)
-        loop(0, nla, one)
-        ts[k] = ssum[...].T
+                ssum[k, 0 : z.wr, :] += zr[k, t].astype(F32)
+        loop(0, chips, one)
+        ts[k] = ssum[k].T
 
         def two(m):
             lb[k, m] = ts[k, pl.ds(pl.multiple_of(m * z.wc, z.wc), z.wc), :].astype(BF)
@@ -533,20 +580,19 @@
         loop(0, nlo, two)
 
     def lon_finish(k):
-        gw[k] = ts[k, pl.ds(pl.multiple_of(lo * z.wc, z.wc), z.wc), :]
+        received(lr.at[k, pl.ds(0, nlo - 1)], ro_r.at[k])
+        grads[k, 0 : z.wc] = ts[k, pl.ds(pl.multiple_of(lo * z.wc, z.wc), z.wc), :]
 
         def one(m):
             @pl.when(m != lo)
             def _():
-                lon_wait(k, m).wait_recv()
-                gw[k] += lr[k, m].astype(F32)
+                grads[k, 0 : z.wc] += lr[k, m].astype(F32)
         loop(0, nlo, one)
 
-    lat_start(SECOND, acc2)
-
+    core_start(SECOND, acc2)
+    chip_start(SECOND)
     sums = jnp.sum(shared(y2, 1), axis=0)
     gain_grad, shift_grad = sums[:, :C], sums[:, C : 2 * C]
-    gv[...] = sums
 
     scale_w = twice(inverse * gain)
     shift_part = twice(shift_grad / total)
@@ -557,63 +603,64 @@
             normed = (act[j, chunk(c), :] - center_w) * inverse_w
             here = cnt[j, chunk(c), :]
             value = sg[j, chunk(c), :] - here * shift_part - here * normed * gain_part
-            low = (scale_w * value * slope[j, chunk(c), :]).astype(BF)
-            F[1 + j, chunk(c), pl.ds(C, W)] = low
+            F[1 + j, chunk(c), own] = (scale_w * value * slope[j, chunk(c), :]).astype(BF)
             return carry
         columns(one, 0)
         halo_send(F, 3, c)
 
     def first_kernel(c):
-        grad = F[1 : 1 + L, chunk(c), pl.ds(C, W)].reshape(L * CH, W)
+        grad = F[1 : 1 + L, chunk(c), own].reshape(L * CH, W)
         kernel_grad(taps(X, c), grad, acc1)
 
     def field_chunk(c):
         halo_wait(F, 3, c)
         out = jnp.dot(taps(F, c), t1[...], preferred_element_type=F32)
         fs[:, chunk(c), :] = out.astype(BF).reshape(L, CH, W)
-        send_out(fs, fo, fo_s, fo_r, c)
-
+
+    def send_field(c):
+        send_out(*field_out, c)
+
+    held = max(nch - 2, 1)
     loop(0, nch, first_grad)
-    loop(0, nch, first_kernel)
-    lat_start(FIRST, acc1)
-    loop(0, nch, field_chunk)
+    first_kernel(0)
+    field_chunk(0)
+    send_field(0)
+    loop(1, nch, first_kernel)
+    core_start(FIRST, acc1)
+    loop(1, held, field_chunk)
+    loop(1, held, send_field)
+    chip_start(FIRST)
+    loop(held, nch, field_chunk)
     lon_start(SECOND)
     lon_start(FIRST)
+    loop(held, nch - 1, send_field)
     lon_finish(SECOND)
     lon_finish(FIRST)
-    square = gw[0] * gw[0] + gw[1] * gw[1]
-    square = total_row(square)
+    first_w, second_w = grads[0, 0 : z.wc], grads[1, 0 : z.wc]
+    square = total_row(first_w * first_w + second_w * second_w)
     share(y3, 2, sum(square[:, cols_of(t)] for t in range(z.LP // C)))
+    loop(max(held, nch - 1), nch, send_field)
     squares = jnp.sum(shared(y3, 2), axis=0)
-    mine2 = total_row((sums * sums).reshape(3, C)) if False else sum(
-        sums[:, cols_of(t)] * sums[:, cols_of(t)] for t in range(3)
-    )
+    mine2 = sum(sums[:, cols_of(t)] * sums[:, cols_of(t)] for t in range(3))
     norm = jnp.sqrt(jnp.sum(squares + mine2, axis=1, keepdims=True))
-    gn[...] = jnp.broadcast_to(norm, (1, C))
-
-    def drain(c):
-        def one(k):
-            f_copy(c, k).wait_send()
-            c_copy(c, k).wait_send()
-            out_copy(bo, ob, bo_s, bo_r, c, k).wait()
-            out_copy(fs, fo, fo_s, fo_r, c, k).wait()
-        loop(1, nlo, one)
-        own_out(bo, ob, bo_s, c).wait()
-        own_out(fs, fo, fo_s, c).wait()
-        for h, ref in enumerate((X, H, G, F)):
-            halo_done(ref, h, c)
-
-    loop(0, nch, drain)
-
-    def drain_lon(k):
-        w_copy(k).wait_send()
-        mask_copy(k).wait_send()
-    loop(1, nlo, drain_lon)
+    for k in range(3):
+        grads[0, z.wc + k : z.wc + k + 1, 0:C] = sums[:, cols_of(k)]
+    grads[0, z.wc + 3 : z.wc + 4, 0:C] = jnp.broadcast_to(norm, (1, C))
+
+    sent(sb.at[:, pl.ds(1, nlo - 1)], f_s.at[0])
+    sent(cb.at[:, pl.ds(1, nlo - 1)], c_s.at[0])
+    sent(wg.at[pl.ds(0, nlo - 1)], wg_s.at[0])
+    sent(cm.at[pl.ds(0, nlo - 1)], mask_s.at[0])
+    for h, ref in enumerate((X, H, G, F)):
+        halo_done(ref, h)
     for k in range(2):
-        loop(1, nla // 2, lambda d: kz_copy(k, d).wait_send())
-        loop(0, nla // 2, lambda d: kc_copy(k, d).wait_send())
-        loop(0, nla, lambda i: pl.when(i != la)(lambda: lat_copy(k, i).wait_send()))
-        loop(0, nlo, lambda m: pl.when(m != lo)(lambda: lon_copy(k, m).wait_send()))
+        sent(kg_in.at[k, pl.ds(0, nla // 2 - 1)], kz_s.at[k])
+        sent(kg_in.at[k, pl.ds(0, nla // 2)], kc_s.at[k])
+        core_copy(k).wait_send()
+        sent(zr.at[k, pl.ds(0, chips - 1)], rz_s.at[k])
+        sent(lr.at[k, pl.ds(0, nlo - 1)], ro_s.at[k])
+    out_done(*block_out)
+    out_done(*field_out)
 
 
 def adam_step(master, first, second, grads, rate, decay):
@@ -627,7 +674,7 @@
 
 def last_kernel(
     z, step,
-    ob, fo, cot, missing, std, gw, gv, gn, wm, wf, wsec, vm, vf, vs,
+    ob, fo, cot, missing, std, grads, wm, wf, wsec, vm, vf, vs,
     block_out, field_grad, norm, w_new, w_first, w_second, w_low, v_new, v_first, v_second,
     cf, bf,
 ):
@@ -646,19 +693,19 @@
 
     @pl.when(pl.program_id(0) == 0)
     def _():
-        size = gn[...]
+        size = grads[0, z.wc + 3 : z.wc + 4, 0:C]
         norm[...] = size[:, 0:1]
         factor = jnp.minimum(1.0, MAX_NORM / size)
         wide = factor[:, 0:1]
         for k in range(2):
-            grads = gw[k, :, 0 : z.wr] * wide
-            new, first, second = adam_step(wm[k], wf[k], wsec[k], grads, RATE_KERNEL, DECAY)
+            own = grads[k, 0 : z.wc, 0 : z.wr] * wide
+            new, first, second = adam_step(wm[k], wf[k], wsec[k], own, RATE_KERNEL, DECAY)
             w_new[k], w_first[k], w_second[k] = new, first, second
             w_low[k] = new.astype(BF)
         for k in range(3):
-            grads = gv[:, cols_of(k)] * factor
+            own = grads[0, z.wc + k : z.wc + k + 1, 0:C] * factor
             row = slice(k, k + 1)
-            new, first, second = adam_step(vm[row, :], vf[row, :], vs[row, :], grads, RATE_VECTOR, 0.0)
+            new, first, second = adam_step(vm[row, :], vf[row, :], vs[row, :], own, RATE_VECTOR, 0.0)
             v_new[row, :], v_first[row, :], v_second[row, :] = new, first, second
 
 
@@ -680,10 +727,12 @@
     V = pltpu.VMEM
     dma = pltpu.SemaphoreType.DMA
     shape = jax.ShapeDtypeStruct
-    padded = V((L + 2, S, 4 * C), BF)
+    padded = V((L + 2, S, 2 * W), BF)
     wide = V((L, S, W), F32)
     scratch = [
-        V(flat, BF), V(flat, BF), V((CH * z.PX, C), F32), V((B, z.PX), F32),
+        V(flat, BF), V(flat, BF), V(sea.shape, sea.dtype), V(miss.shape, miss.dtype),
+        V((1, C), F32), V((1, C), F32), V(wm.shape, F32), V((3, C), F32),
+        V((CH * z.PX, C), F32), V((B, z.PX), F32),
         V((nlo, z.PX, B), F32), wide,
         V((nch, nlo, Q, CH, W), BF), V((nch, nlo, Q, CH, W), BF),
         padded, padded, padded, padded, wide, wide, wide,
@@ -692,23 +741,24 @@
         V((12 * C, W), F32), V((12 * C, W), F32),
         V((2, z.wc, z.LP), BF), V((nlo, 2, z.wc, z.LP), BF), V((2, nla, z.wr, C), BF),
         V((9 * C, C), F32), V((2, z.wr, C), BF),
-        V((2, nla, z.wr, C), BF), V((2, nla, z.wr, C), BF), V((2, 9 * C, C), F32),
-        V((z.LP, C), F32), V((2, C, z.LP), F32), V((2, nlo, z.wc, z.LP), BF), V((2, nlo, z.wc, z.LP), BF),
+        V((2, nla // 2, z.wr, C), BF), V((2, nla // 2, z.wr, C), BF),
+        V((2, nla // 2, z.wr, C), BF), V((2, nla // 2, z.wr, C), BF), V((2, 9 * C, C), F32),
+        V((2, z.LP, C), F32), V((2, C, z.LP), F32), V((2, nlo, z.wc, z.LP), BF), V((2, nlo, z.wc, z.LP), BF),
         V((n, 1, 3 * C), F32), V((n, 1, 3 * C), F32), V((n, 1, C), F32),
-        dma((2,)), dma((nlo,)), dma((nlo,)), dma((nch, nlo)), dma((nch, nlo)),
-        dma((nch, nlo)), dma((nch, nlo)), dma((4, nch, 2)), dma((4, nch, 2)),
-        dma((nch, nlo)), dma((nch, nlo)), dma((nch, nlo)), dma((nch, nlo)),
-        dma((nlo,)), dma((nlo,)), dma((2, nla)), dma((2, nla)), dma((2, nla)), dma((2, nla)),
-        dma((2, nla)), dma((2, nla)), dma((2, nlo)), dma((2, nlo)), dma((3,)), dma((3,)),
+        dma((8,)), dma((1,)), dma((1,)), dma((1,)), dma((nch,)), dma((1,)), dma((nch,)),
+        dma((4,)), dma((4, nch)),
+        dma((1,)), dma((1,)), dma((1,)), dma((1,)), dma((1,)), dma((1,)), dma((1,)), dma((1,)),
+        dma((2,)), dma((2,)), dma((2,)), dma((2,)),
+        dma((2,)), dma((2,)), dma((2,)), dma((2,)), dma((2,)), dma((2,)), dma((3,)), dma((3,)),
     ]
-    ob, fo, gw, gv, gn = pl.pallas_call(
+    ob, fo, grads = pl.pallas_call(
         functools.partial(main_kernel, z),
         out_shape=(
             shape((Q, B, W), BF), shape((Q, B, W), BF),
-            shape((2, z.wc, z.LP), F32), shape((1, 3 * C), F32), shape((1, C), F32),
+            shape((2, z.wc + 8, z.LP), F32),
         ),
-        in_specs=[hbm, hbm] + [vmem] * 6,
-        out_specs=(hbm, hbm, vmem, vmem, vmem),
+        in_specs=[hbm] * 8,
+        out_specs=(hbm, hbm, vmem),
         scratch_shapes=scratch,
         compiler_params=pltpu.CompilerParams(
             collective_id=0, has_side_effects=True, vmem_limit_bytes=56 * 2**20
@@ -731,14 +781,14 @@
         ),
         in_specs=[
             spread, spread, native, pl.BlockSpec((R, Q, step), lambda t: (0, 0, t)), whole((1, C)),
-            whole(gw.shape), whole(gv.shape), whole(gn.shape),
+            whole(grads.shape),
             w_spec, w_spec, w_spec, v_spec, v_spec, v_spec,
         ],
         out_specs=(native, native, whole((1, 1)), w_spec, w_spec, w_spec, w_spec, v_spec, v_spec, v_spec),
         scratch_shapes=[V((step * z.PX, C), F32), V((step * z.PX, C), F32)],
-        compiler_params=pltpu.CompilerParams(vmem_limit_bytes=32 * 2**20),
+        compiler_params=pltpu.CompilerParams(vmem_limit_bytes=60 * 2**20),
         name="update",
-    )(ob, fo, cotangent, miss, std, gw, gv, gn, wm, wf, wsec, vec_master, vec_first, vec_second)
+    )(ob, fo, cotangent, miss, std, grads, wm, wf, wsec, vec_master, vec_first, vec_second)
     block_out, field_grad, norm, w_new, w_f, w_s, w_low, v_new, v_f, v_s = outs
     like = (samples, rows, quads, channels)
     w_new, w_f, w_s, w_low = (jnp.transpose(w, (0, 2, 1)) for w in (w_new, w_f, w_s, w_low))

time: 108 us -> 84.8 us (0.79)
  Pallas kernels: 102 us -> 83.9 us
  local copies, waits for them, and re-layouts: 4.58 us -> 0 us
    pallas_call x1, Pallas kernels: 98.7 us -> 78.6 us  [body(): pl.pallas_call(functools.partial(main_kernel, z), out_shape=(shape((Q, B,...]
    unnamed x28 -> x0, local copies, waits for them, and re-layouts: 4.58 us -> none
    pallas_call x1, Pallas kernels: 3.38 us -> 5.33 us  [body(): pl.pallas_call(functools.partial(last_kernel, z, step), grid=(B // step,)...]
where the time goes in v1:
time: 84.8 us; the launch traced here: 84.6 us
  Pallas kernels  83.9 us (99%)
    pallas_call x1, Pallas kernels, body(): pl.pallas_call(functools.partial(main_kernel, z), out_shape=(shape((Q, B,...  78.6 us
    pallas_call x1, Pallas kernels, body(): pl.pallas_call(functools.partial(last_kernel, z, step), grid=(B // step,)...  5.33 us

profile of v1, /device:TPU:0, one launch (start us, length us, event | category | flops | bytes accessed | tf_op | source)
XLA Modules:
  0.0 84.6 jit_solution(5890845039935124124)
XLA Ops:
  0.6 78.6 %block.1 = (bf16[4,512,256]{2,1,0:T(8,128)(2,1)}, bf16[4,512,256]{2,1,0:T(8,128)(2,1)}, f32[2,40,256]{2,1,0:T(8,128)}) custom-call(bf16[4096,128]{1,0:T(8,128)(2,1)} %bitcast.18, bf16[4096,128]{1,0:T(8,128)(2,1)} %bitcast.16, s32[2,4,512]{2,1,0:T(4,128)} %bitcast.25, s32[2,4,512]{2,1,0:T(4,128)} %bitcast.21, f32[1,128]{1,0:T(1,128)} %bitcast.28, ...), custom_call_target="tpu_custom_call" | custom-call | tf_op jit(solution)/shard_map/block/pallas_call | solution.py:754
  79.3 5.3 %update.1 = (bf16[4096,128]{1,0:T(8,128)(2,1)}, f32[4096,128]{1,0:T(8,128)}, f32[1,1]{1,0:T(1,128)}, f32[2,32,144]{2,1,0:T(8,128)}, f32[2,32,144]{2,1,0:T(8,128)...) custom-call(bf16[4,512,256]{2,1,0:T(8,128)(2,1)} %get-tuple-element., ...), custom_call_target="tpu_custom_call" | custom-call | tf_op jit(solution)/shard_map/update/pallas_call | solution.py:774

commit v2 on v1

--- a/solution.py
+++ b/solution.py
@@ -84,7 +84,7 @@
     fields, cot, sea_h, missing_h, mean_h, std_h, wt_h, vec_h,
     ob, fo, grads,
     fin, cin, sea, missing, mean, std, wt, vec, fb, pres, cm, cnt, sb, cb,
-    X, H, G, F, act, slope, sg, ct, pre, bo, fs,
+    X, H, G, F, act, slope, sg, ct, pre, bo, fs, red,
     w1, w2, t1, t2, acc1, acc2,
     ws, wg, kg_in, kf, kl,
     ca, cr, za, zr, kform, ssum, ts, lb, lr,
@@ -437,6 +437,70 @@
     center_w, inverse_w = twice(center), twice(inverse)
     gain_w, shift_w, bias_w = twice(gain), twice(shift), twice(bias)
 
+    chip, chips = la // 2, nla // 2
+
+    def rows_of(k, i):
+        return kform[k, pl.ds(pl.multiple_of(i * z.wr, 8), z.wr), :]
+
+    def core_copy(k):
+        return remote(ca.at[k], cr.at[k], rc_s.at[k], rc_r.at[k], sibling, lo)
+
+    def core_start(k, acc):
+        for a in range(3):
+            for b in range(3):
+                top, low = (b * 4 + a) * C, (b * 4 + a + 1) * C
+                kform[k, pl.ds((3 * a + b) * C, C), :] = (
+                    acc[pl.ds(top, C), cols_of(0)] + acc[pl.ds(low, C), cols_of(1)]
+                )
+
+        def one(t):
+            ca[k, t] = rows_of(k, 2 * t + 1 - core).astype(BF)
+        loop(0, chips, one)
+        core_copy(k).start()
+
+    def chip_copy(k, t, slot):
+        return remote(za.at[k, t], zr.at[k, slot], rz_s.at[k], rz_r.at[k], 2 * t + core, lo)
+
+    def chip_start(k):
+        core_copy(k).wait_recv()
+        ssum[k] = jnp.zeros_like(ssum[k])
+        ssum[k, 0 : z.wr, :] = rows_of(k, la) + cr[k, chip].astype(F32)
+
+        def one(t):
+            @pl.when(t != chip)
+            def _():
+                za[k, t] = (rows_of(k, 2 * t + core) + cr[k, t].astype(F32)).astype(BF)
+                chip_copy(k, t, chip).start()
+        loop(0, chips, one)
+
+    def lon_copy(k, m):
+        return remote(lb.at[k, m], lr.at[k, lo], ro_s.at[k], ro_r.at[k], la, m)
+
+    def lon_start(k):
+        received(zr.at[k, pl.ds(0, chips - 1)], rz_r.at[k])
+
+        def one(t):
+            @pl.when(t != chip)
+            def _():
+                ssum[k, 0 : z.wr, :] += zr[k, t].astype(F32)
+        loop(0, chips, one)
+        ts[k] = ssum[k].T
+
+        def two(m):
+            lb[k, m] = ts[k, pl.ds(pl.multiple_of(m * z.wc, z.wc), z.wc), :].astype(BF)
+            pl.when(m != lo)(lambda: lon_copy(k, m).start())
+        loop(0, nlo, two)
+
+    def lon_finish(k):
+        received(lr.at[k, pl.ds(0, nlo - 1)], ro_r.at[k])
+        grads[k, 0 : z.wc] = ts[k, pl.ds(pl.multiple_of(lo * z.wc, z.wc), z.wc), :]
+
+        def one(m):
+            @pl.when(m != lo)
+            def _():
+                grads[k, 0 : z.wc] += lr[k, m].astype(F32)
+        loop(0, nlo, one)
+
     def hidden(c):
         def one(j, carry):
             normed = (act[j, chunk(c), :] - center_w) * inverse_w
@@ -473,7 +537,7 @@
     field_out = (fs, fo, fo_s, fo_r, fo_o)
     early = min(1, nch - 1)
 
-    def second_chunk(c, b8):
+    def second_chunk(c):
         halo_wait(H, 1, c)
         received(ct.at[pl.ds(0, Q * (nlo - 1)), chunk(c), :], c_r.at[c])
         conv(taps(H, c), w2)
@@ -486,15 +550,14 @@
             G[1 + j, chunk(c), own] = low
             return carry + to_eight(low.astype(F32))
 
-        b8 = columns(one, b8)
+        red[0] += columns(one, zero8)
         halo_send(G, 2, c)
-        return b8
 
     def second_kernel(c):
         grad = G[1 : 1 + L, chunk(c), own].reshape(L * CH, W)
         kernel_grad(taps(H, c), grad, acc2)
 
-    def back_chunk(c, carry):
+    def back_chunk(c):
         halo_wait(G, 2, c)
         conv(taps(G, c), t2)
 
@@ -505,91 +568,24 @@
             normed = (act[j, chunk(c), :] - center_w) * inverse_w
             return g8 + to_eight(value * normed), s8 + to_eight(value)
 
-        return columns(one, carry)
+        g8, s8 = columns(one, (zero8, zero8))
+        red[1] += g8
+        red[2] += s8
 
     loop(0, nch, hidden)
-    b8 = second_chunk(0, zero8)
-
-    def second_step(c, carry):
-        b8, g8, s8 = carry
-        b8 = second_chunk(c + 1, b8)
+    def second_step(c):
+        second_chunk(c)
         pl.when(c < early)(lambda: send_out(*block_out, c))
-        second_kernel(c)
-        g8, s8 = back_chunk(c, (g8, s8))
-        return b8, g8, s8
-
-    b8, g8, s8 = lax.fori_loop(0, nch - 1, second_step, (b8, zero8, zero8))
-    second_kernel(nch - 1)
-    g8, s8 = back_chunk(nch - 1, (g8, s8))
-    sums = [fold(total_row(v)) for v in (g8, s8, b8)]
+
+    red[...] = jnp.zeros_like(red)
+    loop(0, nch, second_step)
+    loop(0, nch, second_kernel)
+    core_start(SECOND, acc2)
+    loop(0, nch, back_chunk)
+    sums = [fold(total_row(red[k])) for k in (1, 2, 0)]
     share(y2, 1, jnp.concatenate(sums, axis=1))
     loop(early, nch, lambda c: send_out(*block_out, c))
 
-    chip, chips = la // 2, nla // 2
-
-    def rows_of(k, i):
-        return kform[k, pl.ds(pl.multiple_of(i * z.wr, 8), z.wr), :]
-
-    def core_copy(k):
-        return remote(ca.at[k], cr.at[k], rc_s.at[k], rc_r.at[k], sibling, lo)
-
-    def core_start(k, acc):
-        for a in range(3):
-            for b in range(3):
-                top, low = (b * 4 + a) * C, (b * 4 + a + 1) * C
-                kform[k, pl.ds((3 * a + b) * C, C), :] = (
-                    acc[pl.ds(top, C), cols_of(0)] + acc[pl.ds(low, C), cols_of(1)]
-                )
-
-        def one(t):
-            ca[k, t] = rows_of(k, 2 * t + 1 - core).astype(BF)
-        loop(0, chips, one)
-        core_copy(k).start()
-
-    def chip_copy(k, t, slot):
-        return remote(za.at[k, t], zr.at[k, slot], rz_s.at[k], rz_r.at[k], 2 * t + core, lo)
-
-    def chip_start(k):
-        core_copy(k).wait_recv()
-        ssum[k] = jnp.zeros_like(ssum[k])
-        ssum[k, 0 : z.wr, :] = rows_of(k, la) + cr[k, chip].astype(F32)
-
-        def one(t):
-            @pl.when(t != chip)
-            def _():
-                za[k, t] = (rows_of(k, 2 * t + core) + cr[k, t].astype(F32)).astype(BF)
-                chip_copy(k, t, chip).start()
-        loop(0, chips, one)
-
-    def lon_copy(k, m):
-        return remote(lb.at[k, m], lr.at[k, lo], ro_s.at[k], ro_r.at[k], la, m)
-
-    def lon_start(k):
-        received(zr.at[k, pl.ds(0, chips - 1)], rz_r.at[k])
-
-        def one(t):
-            @pl.when(t != chip)
-            def _():
-                ssum[k, 0 : z.wr, :] += zr[k, t].astype(F32)
-        loop(0, chips, one)
-        ts[k] = ssum[k].T
-
-        def two(m):
-            lb[k, m] = ts[k, pl.ds(pl.multiple_of(m * z.wc, z.wc), z.wc), :].astype(BF)
-            pl.when(m != lo)(lambda: lon_copy(k, m).start())
-        loop(0, nlo, two)
-
-    def lon_finish(k):
-        received(lr.at[k, pl.ds(0, nlo - 1)], ro_r.at[k])
-        grads[k, 0 : z.wc] = ts[k, pl.ds(pl.multiple_of(lo * z.wc, z.wc), z.wc), :]
-
-        def one(m):
-            @pl.when(m != lo)
-            def _():
-                grads[k, 0 : z.wc] += lr[k, m].astype(F32)
-        loop(0, nlo, one)
-
-    core_start(SECOND, acc2)
     chip_start(SECOND)
     sums = jnp.sum(shared(y2, 1), axis=0)
     gain_grad, shift_grad = sums[:, :C], sums[:, C : 2 * C]
@@ -621,16 +617,15 @@
         send_out(*field_out, c)
 
     held = max(nch - 2, 1)
+    def field_step(c):
+        field_chunk(c)
+        pl.when(c < held)(lambda: send_field(c))
+        pl.when(c == 1)(lambda: chip_start(FIRST))
+
     loop(0, nch, first_grad)
-    first_kernel(0)
-    field_chunk(0)
-    send_field(0)
-    loop(1, nch, first_kernel)
+    loop(0, nch, first_kernel)
     core_start(FIRST, acc1)
-    loop(1, held, field_chunk)
-    loop(1, held, send_field)
-    chip_start(FIRST)
-    loop(held, nch, field_chunk)
+    loop(0, nch, field_step)
     lon_start(SECOND)
     lon_start(FIRST)
     loop(held, nch - 1, send_field)
@@ -736,7 +731,7 @@
         V((nlo, z.PX, B), F32), wide,
         V((nch, nlo, Q, CH, W), BF), V((nch, nlo, Q, CH, W), BF),
         padded, padded, padded, padded, wide, wide, wide,
-        V((L, S, W), BF), V((L, CH, W), F32), V((L, S, W), BF), V((L, S, W), BF),
+        V((L, S, W), BF), V((L, CH, W), F32), V((L, S, W), BF), V((L, S, W), BF), V((3, 8, W), F32),
         V((12 * C, W), BF), V((12 * C, W), BF), V((12 * C, W), BF), V((12 * C, W), BF),
         V((12 * C, W), F32), V((12 * C, W), F32),
         V((2, z.wc, z.LP), BF), V((nlo, 2, z.wc, z.LP), BF), V((2, nla, z.wr, C), BF),

time: 84.8 us -> 78.1 us (0.921)
  Pallas kernels: 83.9 us -> 77.2 us
    pallas_call x1, Pallas kernels: 78.6 us -> 71.8 us  [body(): pl.pallas_call(functools.partial(main_kernel, z), out_shape=(shape((Q, B,...]
where the time goes in v2:
time: 78.1 us; the launch traced here: 77.8 us
  Pallas kernels  77.2 us (99%)
    pallas_call x1, Pallas kernels, body(): pl.pallas_call(functools.partial(main_kernel, z), out_shape=(shape((Q, B,...  71.8 us
    pallas_call x1, Pallas kernels, body(): pl.pallas_call(functools.partial(last_kernel, z, step), grid=(B // step,)...  5.33 us

profile of v2, /device:TPU:0, one launch (start us, length us, event | category | flops | bytes accessed | tf_op | source)
XLA Modules:
  0.0 77.8 jit_solution(10922787844440902058)
XLA Ops:
  0.6 71.8 %block.1 = (bf16[4,512,256]{2,1,0:T(8,128)(2,1)}, bf16[4,512,256]{2,1,0:T(8,128)(2,1)}, f32[2,40,256]{2,1,0:T(8,128)}) custom-call(bf16[4096,128]{1,0:T(8,128)(2,1)} %bitcast.18, bf16[4096,128]{1,0:T(8,128)(2,1)} %bitcast.16, s32[2,4,512]{2,1,0:T(4,128)} %bitcast.25, s32[2,4,512]{2,1,0:T(4,128)} %bitcast.21, f32[1,128]{1,0:T(1,128)} %bitcast.28, ...), custom_call_target="tpu_custom_call" | custom-call | tf_op jit(solution)/shard_map/block/pallas_call | solution.py:749
  72.5 5.3 %update.1 = (bf16[4096,128]{1,0:T(8,128)(2,1)}, f32[4096,128]{1,0:T(8,128)}, f32[1,1]{1,0:T(1,128)}, f32[2,32,144]{2,1,0:T(8,128)}, f32[2,32,144]{2,1,0:T(8,128)...) custom-call(bf16[4,512,256]{2,1,0:T(8,128)(2,1)} %get-tuple-element., ...), custom_call_target="tpu_custom_call" | custom-call | tf_op jit(solution)/shard_map/update/pallas_call | solution.py:769

commit v3 on v2

--- a/solution.py
+++ b/solution.py
@@ -82,8 +82,8 @@
 def main_kernel(
     z,
     fields, cot, sea_h, missing_h, mean_h, std_h, wt_h, vec_h,
-    ob, fo, grads,
-    fin, cin, sea, missing, mean, std, wt, vec, fb, pres, cm, cnt, sb, cb,
+    out_low, out_grad, grads,
+    ob, fo, fin, cin, sea, missing, mean, std, wt, vec, fb, pres, cm, cnt, sb, cb,
     X, H, G, F, act, slope, sg, ct, pre, bo, fs, red,
     w1, w2, t1, t2, acc1, acc2,
     ws, wg, kg_in, kf, kl,
@@ -514,24 +514,51 @@
         return remote(
             src.at[pl.ds(Q * m, Q), chunk(c), :],
             dst.at[:, pl.ds(pl.multiple_of(lo * S + c * CH, CH), CH), :],
-            ss.at[0], rs.at[0], la, m,
+            ss.at[0], rs.at[c], la, m,
         )
 
     def own_out(src, dst, os, c):
         return pltpu.make_async_copy(
             src.at[pl.ds(Q * lo, Q), chunk(c), :],
             dst.at[:, pl.ds(pl.multiple_of(lo * S + c * CH, CH), CH), :],
-            os.at[0],
+            os.at[c],
         )
 
     def send_out(src, dst, ss, rs, os, c):
         loop(1, nlo, lambda k: out_copy(src, dst, ss, rs, c, k).start())
         own_out(src, dst, os, c).start()
 
-    def out_done(src, dst, ss, rs, os):
-        sent(src.at[pl.ds(0, Q * (nlo - 1))], ss.at[0])
-        received(dst.at[:, pl.ds(0, S * (nlo - 1)), :], rs.at[0])
-        pltpu.make_async_copy(src.at[pl.ds(0, Q)], dst.at[:, pl.ds(0, S), :], os.at[0]).wait()
+    def out_arrived(src, dst, rs, os, c):
+        received(dst.at[:, pl.ds(0, CH * (nlo - 1)), :], rs.at[c])
+        pltpu.make_async_copy(src.at[pl.ds(0, Q), chunk(0), :], dst.at[:, chunk(0), :], os.at[c]).wait()
+
+    def native_rows(t, c):
+        first = pl.multiple_of((t * S + c * CH) * z.PX, CH * z.PX)
+        return pl.ds(first, CH * z.PX), pl.ds(pl.multiple_of(t * S + c * CH, CH), CH)
+
+    def finish_block(c):
+        out_arrived(bo, ob, bo_r, bo_o, c)
+
+        def one(t):
+            rows, here = native_rows(t, c)
+            for p in range(z.PX):
+                fb[pl.ds(p, CH, stride=z.PX), :] = ob[p % Q, here, cols_of(p // Q)].astype(F32)
+            out_low[rows, :] = fb[...].astype(BF)
+        loop(0, nlo, one)
+
+    def finish_field(c):
+        out_arrived(fs, fo, fo_r, fo_o, c)
+
+        def one(t):
+            rows, here = native_rows(t, c)
+            fb[...] = cin[rows, :].astype(F32)
+            have = pres[here, :]
+            for p in range(z.PX):
+                pixel = pl.ds(p, CH, stride=z.PX)
+                grad = fb[pixel, :] + fo[p % Q, here, cols_of(p // Q)].astype(F32)
+                fb[pixel, :] = grad * have[:, p : p + 1] * rstd
+            out_grad[rows, :] = fb[...]
+        loop(0, nlo, one)
 
     block_out = (bo, ob, bo_s, bo_r, bo_o)
     field_out = (fs, fo, fo_s, fo_r, fo_o)
@@ -629,18 +656,22 @@
     lon_start(SECOND)
     lon_start(FIRST)
     loop(held, nch - 1, send_field)
+    loop(0, nch, finish_block)
     lon_finish(SECOND)
     lon_finish(FIRST)
     first_w, second_w = grads[0, 0 : z.wc], grads[1, 0 : z.wc]
     square = total_row(first_w * first_w + second_w * second_w)
     share(y3, 2, sum(square[:, cols_of(t)] for t in range(z.LP // C)))
     loop(max(held, nch - 1), nch, send_field)
+    loop(0, nch - 1, finish_field)
     squares = jnp.sum(shared(y3, 2), axis=0)
     mine2 = sum(sums[:, cols_of(t)] * sums[:, cols_of(t)] for t in range(3))
     norm = jnp.sqrt(jnp.sum(squares + mine2, axis=1, keepdims=True))
     for k in range(3):
         grads[0, z.wc + k : z.wc + k + 1, 0:C] = sums[:, cols_of(k)]
     grads[0, z.wc + 3 : z.wc + 4, 0:C] = jnp.broadcast_to(norm, (1, C))
+
+    finish_field(nch - 1)
 
     sent(sb.at[:, pl.ds(1, nlo - 1)], f_s.at[0])
     sent(cb.at[:, pl.ds(1, nlo - 1)], c_s.at[0])
@@ -654,8 +685,8 @@
         core_copy(k).wait_send()
         sent(zr.at[k, pl.ds(0, chips - 1)], rz_s.at[k])
         sent(lr.at[k, pl.ds(0, nlo - 1)], ro_s.at[k])
-    out_done(*block_out)
-    out_done(*field_out)
+    sent(bo.at[pl.ds(0, Q * (nlo - 1))], bo_s.at[0])
+    sent(fs.at[pl.ds(0, Q * (nlo - 1))], fo_s.at[0])
 
 
 def adam_step(master, first, second, grads, rate, decay):
@@ -668,40 +699,43 @@
 
 
 def last_kernel(
-    z, step,
-    ob, fo, cot, missing, std, grads, wm, wf, wsec, vm, vf, vs,
-    block_out, field_grad, norm, w_new, w_first, w_second, w_low, v_new, v_first, v_second,
-    cf, bf,
+    z,
+    low, grad, grads, wm_h, wf_h, ws_h, vm_h, vf_h, vs_h,
+    block_out, field_grad, norm_h, w_new_h, w_first_h, w_second_h, w_low_h, v_new_h, v_first_h, v_second_h,
+    wm, wf, wsec, vm, vf, vs, norm, w_new, w_first, w_second, w_low, v_new, v_first, v_second,
+    in_sem, out_sem,
 ):
-    Q = z.Q
-    present, _ = both_masks(missing[...], None)
-    have = present.T
-    rstd = 1.0 / std[...]
-    cf[...] = cot[...].astype(F32)
-    for p in range(z.PX):
-        i, q = p // Q, p % Q
-        here = pl.ds(p, step, stride=z.PX)
-        grad = cf[here, :] + fo[q, :, cols_of(i)].astype(F32)
-        field_grad[here, :] = grad * have[:, p : p + 1] * rstd
-        bf[here, :] = ob[q, :, cols_of(i)].astype(F32)
-    block_out[...] = bf[...].astype(BF)
-
-    @pl.when(pl.program_id(0) == 0)
-    def _():
-        size = grads[0, z.wc + 3 : z.wc + 4, 0:C]
-        norm[...] = size[:, 0:1]
-        factor = jnp.minimum(1.0, MAX_NORM / size)
-        wide = factor[:, 0:1]
-        for k in range(2):
-            own = grads[k, 0 : z.wc, 0 : z.wr] * wide
-            new, first, second = adam_step(wm[k], wf[k], wsec[k], own, RATE_KERNEL, DECAY)
-            w_new[k], w_first[k], w_second[k] = new, first, second
-            w_low[k] = new.astype(BF)
-        for k in range(3):
-            own = grads[0, z.wc + k : z.wc + k + 1, 0:C] * factor
-            row = slice(k, k + 1)
-            new, first, second = adam_step(vm[row, :], vf[row, :], vs[row, :], own, RATE_VECTOR, 0.0)
-            v_new[row, :], v_first[row, :], v_second[row, :] = new, first, second
+    ins = ((wm_h, wm), (wf_h, wf), (ws_h, wsec), (vm_h, vm), (vf_h, vf), (vs_h, vs))
+    loads = [pltpu.make_async_copy(src, dst, in_sem.at[i]) for i, (src, dst) in enumerate(ins)]
+    for load in loads:
+        load.start()
+    outs = (
+        (grad, field_grad), (low, block_out), (norm, norm_h), (w_new, w_new_h), (w_first, w_first_h),
+        (w_second, w_second_h), (w_low, w_low_h), (v_new, v_new_h), (v_first, v_first_h), (v_second, v_second_h),
+    )
+    stores = [pltpu.make_async_copy(src, dst, out_sem.at[i]) for i, (src, dst) in enumerate(outs)]
+    stores[0].start()
+    stores[1].start()
+    size = grads[0, z.wc + 3 : z.wc + 4, 0:C]
+    norm[...] = size[:, 0:1]
+    factor = jnp.minimum(1.0, MAX_NORM / size)
+    wide = factor[:, 0:1]
+    for load in loads:
+        load.wait()
+    for k in range(2):
+        own = grads[k, 0 : z.wc, 0 : z.wr] * wide
+        new, first, second = adam_step(wm[k], wf[k], wsec[k], own, RATE_KERNEL, DECAY)
+        w_new[k], w_first[k], w_second[k] = new, first, second
+        w_low[k] = new.astype(BF)
+    for k in range(3):
+        own = grads[0, z.wc + k : z.wc + k + 1, 0:C] * factor
+        row = slice(k, k + 1)
+        new, first, second = adam_step(vm[row, :], vf[row, :], vs[row, :], own, RATE_VECTOR, 0.0)
+        v_new[row, :], v_first[row, :], v_second[row, :] = new, first, second
+    for store in stores[2:]:
+        store.start()
+    for store in stores:
+        store.wait()
 
 
 def body(nla, nlo, fields, chan_mean, chan_std, sea_mask, missing, cotangent,
@@ -725,7 +759,7 @@
     padded = V((L + 2, S, 2 * W), BF)
     wide = V((L, S, W), F32)
     scratch = [
-        V(flat, BF), V(flat, BF), V(sea.shape, sea.dtype), V(miss.shape, miss.dtype),
+        V((Q, B, W), BF), V((Q, B, W), BF), V(flat, BF), V(flat, BF), V(sea.shape, sea.dtype), V(miss.shape, miss.dtype),
         V((1, C), F32), V((1, C), F32), V(wm.shape, F32), V((3, C), F32),
         V((CH * z.PX, C), F32), V((B, z.PX), F32),
         V((nlo, z.PX, B), F32), wide,
@@ -742,48 +776,33 @@
         V((n, 1, 3 * C), F32), V((n, 1, 3 * C), F32), V((n, 1, C), F32),
         dma((8,)), dma((1,)), dma((1,)), dma((1,)), dma((nch,)), dma((1,)), dma((nch,)),
         dma((4,)), dma((4, nch)),
-        dma((1,)), dma((1,)), dma((1,)), dma((1,)), dma((1,)), dma((1,)), dma((1,)), dma((1,)),
+        dma((1,)), dma((nch,)), dma((nch,)), dma((1,)), dma((nch,)), dma((nch,)), dma((1,)), dma((1,)),
         dma((2,)), dma((2,)), dma((2,)), dma((2,)),
         dma((2,)), dma((2,)), dma((2,)), dma((2,)), dma((2,)), dma((2,)), dma((3,)), dma((3,)),
     ]
-    ob, fo, grads = pl.pallas_call(
+    low, grad, grads = pl.pallas_call(
         functools.partial(main_kernel, z),
-        out_shape=(
-            shape((Q, B, W), BF), shape((Q, B, W), BF),
-            shape((2, z.wc + 8, z.LP), F32),
-        ),
+        out_shape=(V(flat, BF), V(flat, F32), V((2, z.wc + 8, z.LP), F32)),
         in_specs=[hbm] * 8,
-        out_specs=(hbm, hbm, vmem),
+        out_specs=(vmem, vmem, vmem),
         scratch_shapes=scratch,
         compiler_params=pltpu.CompilerParams(
-            collective_id=0, has_side_effects=True, vmem_limit_bytes=56 * 2**20
+            collective_id=0, has_side_effects=True, vmem_limit_bytes=59 * 2**20
         ),
         name="block",
     )(fields, cotangent, sea, miss, mean, std, wm, vec_master)
 
-    step = min(128, B)
-    whole = lambda s: pl.BlockSpec(s, lambda t: (0,) * len(s))
-    native = pl.BlockSpec((step * z.PX, C), lambda t: (t, 0))
-    spread = pl.BlockSpec((Q, step, W), lambda t: (0, t, 0))
-    w_spec, v_spec = whole(wm.shape), whole((3, C))
+    shapes = [((1, 1), F32)] + [(wm.shape, F32)] * 3 + [(wm.shape, BF)] + [((3, C), F32)] * 3
     outs = pl.pallas_call(
-        functools.partial(last_kernel, z, step),
-        grid=(B // step,),
-        out_shape=(
-            shape(flat, BF), shape(flat, F32), shape((1, 1), F32),
-            shape(wm.shape, F32), shape(wm.shape, F32), shape(wm.shape, F32), shape(wm.shape, BF),
-            shape((3, C), F32), shape((3, C), F32), shape((3, C), F32),
-        ),
-        in_specs=[
-            spread, spread, native, pl.BlockSpec((R, Q, step), lambda t: (0, 0, t)), whole((1, C)),
-            whole(grads.shape),
-            w_spec, w_spec, w_spec, v_spec, v_spec, v_spec,
-        ],
-        out_specs=(native, native, whole((1, 1)), w_spec, w_spec, w_spec, w_spec, v_spec, v_spec, v_spec),
-        scratch_shapes=[V((step * z.PX, C), F32), V((step * z.PX, C), F32)],
-        compiler_params=pltpu.CompilerParams(vmem_limit_bytes=60 * 2**20),
+        functools.partial(last_kernel, z),
+        out_shape=[shape(flat, BF), shape(flat, F32)] + [shape(*v) for v in shapes],
+        in_specs=[vmem] * 3 + [hbm] * 6,
+        out_specs=[hbm] * 10,
+        scratch_shapes=[V(wm.shape, F32)] * 3 + [V((3, C), F32)] * 3 + [V(*v) for v in shapes]
+        + [dma((6,)), dma((10,))],
+        compiler_params=pltpu.CompilerParams(vmem_limit_bytes=16 * 2**20),
         name="update",
-    )(ob, fo, cotangent, miss, std, grads, wm, wf, wsec, vec_master, vec_first, vec_second)
+    )(low, grad, grads, wm, wf, wsec, vec_master, vec_first, vec_second)
     block_out, field_grad, norm, w_new, w_f, w_s, w_low, v_new, v_f, v_s = outs
     like = (samples, rows, quads, channels)
     w_new, w_f, w_s, w_low = (jnp.transpose(w, (0, 2, 1)) for w in (w_new, w_f, w_s, w_low))

time: 78.1 us -> 74.9 us (0.959)
  Pallas kernels: 77.2 us -> 73.9 us
    pallas_call x2, Pallas kernels: 77.2 us -> 73.9 us  [the longest x1 71.8 us: body(): pl.pallas_call(functools.partial(main_kernel, z), out_shape=(V(flat, BF),...]
where the time goes in v3:
time: 74.9 us; the launch traced here: 74.7 us
  Pallas kernels  73.9 us (99%)
  between operations  0.75 us (1%)
    pallas_call x1, Pallas kernels, body(): pl.pallas_call(functools.partial(main_kernel, z), out_shape=(V(flat, BF),...  71.8 us
    pallas_call x1, Pallas kernels, body(): pl.pallas_call(functools.partial(last_kernel, z), out_shape=[shape(flat,...  2.13 us

profile of v3, /device:TPU:0, one launch (start us, length us, event | category | flops | bytes accessed | tf_op | source)
XLA Modules:
  0.0 74.7 jit_solution(17607686987852108438)
XLA Ops:
  0.6 0.0 copy-start.3
  0.7 0.0 copy-start.5
  0.7 0.0 copy-start.4
  0.7 0.0 copy-start.2
  0.7 0.0 copy-start.1
  0.7 0.0 copy-start
  0.7 71.8 %block.1 = (bf16[4096,128]{1,0:T(8,128)(2,1)S(1)}, f32[4096,128]{1,0:T(8,128)S(1)}, f32[2,40,256]{2,1,0:T(8,128)S(1)}) custom-call(bf16[4096,128]{1,0:T(8,128)(2,1)} %bitcast.20, bf16[4096,128]{1,0:T(8,128)(2,1)} %bitcast.21, s32[2,4,512]{2,1,0:T(4,128)} %bitcast.22, s32[2,4,512]{2,1,0:T(4,128)} %bitcast.23, f32[1,128]{1,0:T(1,128)} %bitcast.24, ...), custom_call_target="tpu_custom_call" | custom-call | tf_op jit(solution)/shard_map/block/pallas_call | solution.py:783
  72.5 0.0 copy-done.3
  72.5 0.0 copy-done.5
  72.6 0.0 copy-done.4
  72.6 0.0 copy-done.2
  72.6 0.0 copy-done.1
  72.6 0.0 copy-done
  72.6 2.1 %update.1 = (bf16[4096,128]{1,0:T(8,128)(2,1)}, f32[4096,128]{1,0:T(8,128)}, f32[1,1]{1,0:T(1,128)}, f32[2,32,144]{2,1,0:T(8,128)}, f32[2,32,144]{2,1,0:T(8,128)...) custom-call(bf16[4096,128]{1,0:T(8,128)(2,1)S(1)} %get-tuple-element, ...), custom_call_target="tpu_custom_call" | custom-call | tf_op jit(solution)/shard_map/update/pallas_call | solution.py:796
Async XLA Ops:
  0.6 71.9 %copy-start.3 = (f32[3,128]{1,0:T(4,128)S(1)}, f32[3,128]{1,0:T(4,128)}, u32[]{:S(2)}) copy-start(f32[3,128]{1,0:T(4,128)} %vm_h.1) | copy-start | bytes 4612
  0.7 71.9 %copy-start.5 = (f32[3,128]{1,0:T(4,128)S(1)}, f32[3,128]{1,0:T(4,128)}, u32[]{:S(2)}) copy-start(f32[3,128]{1,0:T(4,128)} %vs_h.1) | copy-start | bytes 4612
  0.7 71.9 %copy-start.4 = (f32[3,128]{1,0:T(4,128)S(1)}, f32[3,128]{1,0:T(4,128)}, u32[]{:S(2)}) copy-start(f32[3,128]{1,0:T(4,128)} %vf_h.1) | copy-start | bytes 4612
  0.7 71.9 %copy-start.2 = (f32[2,144,32]{1,2,0:T(8,128)S(1)}, f32[2,144,32]{1,2,0:T(8,128)}, u32[]{:S(2)}) copy-start(f32[2,144,32]{1,2,0:T(8,128)} %param.20) | copy-start | bytes 110596
  0.7 71.9 %copy-start.1 = (f32[2,144,32]{1,2,0:T(8,128)S(1)}, f32[2,144,32]{1,2,0:T(8,128)}, u32[]{:S(2)}) copy-start(f32[2,144,32]{1,2,0:T(8,128)} %param.19) | copy-start | bytes 110596
  0.7 71.9 %copy-start = (f32[2,144,32]{1,2,0:T(8,128)S(1)}, f32[2,144,32]{1,2,0:T(8,128)}, u32[]{:S(2)}) copy-start(f32[2,144,32]{1,2,0:T(8,128)} %param.18) | copy-start | bytes 110596

commit v4 on v3

--- a/solution.py
+++ b/solution.py
@@ -83,15 +83,16 @@
     z,
     fields, cot, sea_h, missing_h, mean_h, std_h, wt_h, vec_h,
     out_low, out_grad, grads,
-    ob, fo, fin, cin, sea, missing, mean, std, wt, vec, fb, pres, cm, cnt, sb, cb,
+    ob, fo, fin, cin, sea, missing, mean, std, wt, vec, fb, pres, cmo, cm, cmn, cnt, sb, cb,
     X, H, G, F, act, slope, sg, ct, pre, bo, fs, red,
+    p_o, p_h, sg_o, sg_h, act_h, slope_h, cnt_h,
     w1, w2, t1, t2, acc1, acc2,
     ws, wg, kg_in, kf, kl,
     ca, cr, za, zr, kform, ssum, ts, lb, lr,
     y1, y2, y3,
     load_sem, mask_s, mask_r, f_s, f_r, c_s, c_r, halo_s, halo_r,
     bo_s, bo_r, bo_o, fo_s, fo_r, fo_o, wg_s, wg_r, kz_s, kz_r, kc_s, kc_r,
-    rc_s, rc_r, rz_s, rz_r, ro_s, ro_r, y_s, y_r,
+    rc_s, rc_r, rz_s, rz_r, ro_s, ro_r, y_s, y_r, near_s, near_r,
 ):
     nla, nlo, n = z.nla, z.nlo, z.n
     S, L, Q, CH, nch = z.S, z.L, z.Q, z.CH, z.nch
@@ -152,30 +153,36 @@
 
     present, counted = both_masks(missing[...], sea[...])
     pres[...] = present.T
-    cm[lo] = counted
+    width = min(z.B, 128)
+
+    def for_lon(m):
+        return pltpu.roll(counted, lax.rem(z.B - m * S, z.B), 1)[:, :width]
+
+    for k in range(1, nlo):
+        cmo[k] = for_lon(peer(k))
+    cm[lo] = for_lon(lo)
     pad = z.LP - z.wr
     for k in range(2):
         block = wt[k].astype(BF)
         if pad:
             block = jnp.concatenate([block, jnp.zeros((z.wc, pad), BF)], axis=1)
         ws[k] = block
-        wg[lo, k] = block
+        wg[k, lo] = block
     north_pole, south_pole = la == 0, la == nla - 1
-    for ref in (X, H, G, F):
-        @pl.when(north_pole)
+    for side, pole in enumerate((north_pole, south_pole)):
+        @pl.when(pole)
         def _():
-            ref[:, :, cols_of(0)] = jnp.zeros((L + 2, S, C), BF)
-
-        @pl.when(south_pole)
-        def _():
-            ref[:, :, cols_of(3)] = jnp.zeros((L + 2, S, C), BF)
-
-    def w_copy(k):
-        m = peer(k)
-        return remote(ws, wg.at[lo], wg_s.at[0], wg_r.at[0], la, m)
+            for ref in (X, G):
+                ref[:, :, cols_of(3 * side)] = jnp.zeros((L + 2, S, C), BF)
+            for ref in (p_h, sg_h):
+                ref[:, :, cols_of(side)] = jnp.zeros((L, S, C), BF)
+            cmn[side] = jnp.zeros_like(cm)
+
+    def w_copy(kind, k):
+        return remote(ws.at[kind], wg.at[kind, lo], wg_s.at[kind], wg_r.at[kind], la, peer(k))
 
     def mask_copy(k):
-        return remote(cm.at[lo], cm.at[lo], mask_s.at[0], mask_r.at[0], la, peer(k))
+        return remote(cmo.at[k], cm.at[lo], mask_s.at[0], mask_r.at[0], la, peer(k))
 
     load_f.wait()
 
@@ -237,16 +244,12 @@
 
     prep_fields(0)
     pl.semaphore_wait(barrier, n - 1)
-    loop(1, nlo, lambda k: w_copy(k).start())
+    loop(1, nlo, lambda k: w_copy(FIRST, k).start())
     loop(1, nlo, lambda k: mask_copy(k).start())
     send_fields(0)
+    loop(1, nlo, lambda k: w_copy(SECOND, k).start())
     loop(1, nch, next_fields)
 
-    received(wg.at[pl.ds(0, nlo - 1)], wg_r.at[0])
-    for k in range(2):
-        gathered = jnp.concatenate([wg[m, k].astype(F32) for m in range(nlo)], axis=0)
-        kl[k] = gathered.T[: z.wr].astype(BF)
-        kg_in[k, la] = kl[k]
     core = lax.rem(la, 2)
     sibling = la + 1 - 2 * core
 
@@ -259,6 +262,10 @@
         return remote(kg_in.at[k, row], kg_in.at[k, row], kc_s.at[k], kc_r.at[k], sibling, lo)
 
     def start_kernel(k):
+        received(wg.at[k, pl.ds(0, nlo - 1)], wg_r.at[k])
+        gathered = jnp.concatenate([wg[k, m].astype(F32) for m in range(nlo)], axis=0)
+        kl[k] = gathered.T[: z.wr].astype(BF)
+        kg_in[k, la] = kl[k]
         loop(1, nla // 2, lambda d: kz_copy(k, d).start())
         kc_copy(k, 0).start()
 
@@ -293,29 +300,56 @@
                 ref[pl.ds((b * 4 + r) * C, C), cols_of(i)] = jnp.zeros((C, C), BF)
 
     start_kernel(FIRST)
-    start_kernel(SECOND)
 
     loop(0, nch, own_fields)
     load_c.wait()
     loop(0, nch, own_cot)
     loop(0, nch, prep_cot)
+    start_kernel(SECOND)
 
     def spread_mask():
-        rows = jnp.concatenate([cm[m] for m in range(nlo)], axis=0)
-        back = z.B - lo * S
-        mine = pltpu.roll(rows, lax.rem(back, z.B), 1)[:, : min(z.B, 128)].T
+        mine = jnp.concatenate([cm[m] for m in range(nlo)], axis=0).T
         for j in range(L):
             for i in range(R):
                 col = (j // Q) * z.PX + i * Q + j % Q
                 cnt[j, :, cols_of(i)] = jnp.broadcast_to(mine[:S, col : col + 1], (S, C))
 
+    def spread_near():
+        for side in range(2):
+            theirs = jnp.concatenate([cmn[side, m] for m in range(nlo)], axis=0).T
+            for j in range(L):
+                col = (j // Q) * z.PX + (1 - side) * Q + j % Q
+                cnt_h[j, :, cols_of(side)] = jnp.broadcast_to(theirs[:S, col : col + 1], (S, C))
+
+    def near_copy(side):
+        to = jnp.maximum(la - 1, 0) if side == 0 else jnp.minimum(la + 1, nla - 1)
+        return remote(cm, cmn.at[1 - side], near_s.at[side], near_r.at[side], to, lo)
+
     def halo_copies(ref, h, c):
         def lanes(r):
             return ref.at[pl.ds(1, L), chunk(c), pl.ds(r * C, C)]
 
-        north = remote(lanes(1), lanes(3), halo_s.at[h], halo_r.at[h, c], jnp.maximum(la - 1, 0), lo)
-        south = remote(lanes(2), lanes(0), halo_s.at[h], halo_r.at[h, c], jnp.minimum(la + 1, nla - 1), lo)
+        return pair(lanes(1), lanes(3), lanes(2), lanes(0), h, c)
+
+    def pair(up_from, up_to, down_from, down_to, h, c):
+        north = remote(up_from, up_to, halo_s.at[h], halo_r.at[h, c], jnp.maximum(la - 1, 0), lo)
+        south = remote(down_from, down_to, halo_s.at[h], halo_r.at[h, c], jnp.minimum(la + 1, nla - 1), lo)
         return north, south
+
+    def edge_send(src, dst, h, c):
+        def lanes(ref, side):
+            return ref.at[:, chunk(c), pl.ds(side * C, C)]
+        north, south = pair(lanes(src, 0), lanes(dst, 1), lanes(src, 1), lanes(dst, 0), h, c)
+        pl.when(la > 0)(north.start)
+        pl.when(la < nla - 1)(south.start)
+
+    def edge_wait(ref, h, c):
+        pl.when(at_pole)(lambda: received(ref.at[:, chunk(c), pl.ds(0, C)], halo_r.at[h, c]))
+        pl.when(jnp.logical_not(at_pole))(lambda: received(ref.at[:, chunk(c), :], halo_r.at[h, c]))
+
+    def edge_done(ref, h):
+        pl.when(at_pole)(lambda: sent(ref.at[:, :, pl.ds(0, C)], halo_s.at[h]))
+        pl.when(jnp.logical_not(at_pole))(lambda: sent(ref, halo_s.at[h]))
 
     def halo_send(ref, h, c):
         north, south = halo_copies(ref, h, c)
@@ -329,6 +363,9 @@
             received(ref.at[pl.ds(1, L), chunk(c), pl.ds(0, width)], halo_r.at[h, c])
         pl.when(at_pole)(lambda: both(C))
         pl.when(jnp.logical_not(at_pole))(lambda: both(W))
+        wrap(ref, c)
+
+    def wrap(ref, c):
         ref[0, chunk(c), :] = ref[L, chunk(c), :]
         ref[L + 1, chunk(c), :] = ref[1, chunk(c), :]
 
@@ -366,6 +403,7 @@
 
         def one(j, carry):
             s, m = carry
+            p_o[j, chunk(c), :] = pre[j].astype(BF)
             value, grad = smooth(pre[j])
             act[j, chunk(c), :] = value
             slope[j, chunk(c), :] = grad
@@ -388,12 +426,22 @@
         m_1 = m_0 + m_c + delta * delta * (n_0 * n_c / jnp.maximum(n_1, 1.0))
         return n_1, s_0 + s_c, m_1
 
+    def first_edge(c):
+        edge_wait(p_h, 1, c)
+
+        def one(j, carry):
+            act_h[j, chunk(c), :], slope_h[j, chunk(c), :] = smooth(p_h[j, chunk(c), :].astype(F32))
+            return carry
+        columns(one, 0)
+
     def send_cot(c):
         loop(1, nlo, lambda k: c_copy(c, k).start())
 
     arrive(0)
     forward_kernel(FIRST)
     received(cm.at[pl.ds(0, nlo - 1)], mask_r.at[0])
+    for side, pole in enumerate((north_pole, south_pole)):
+        pl.when(jnp.logical_not(pole))(lambda: near_copy(side).start())
     spread_mask()
     finish_kernel(FIRST)
     build_forward(w1)
@@ -418,8 +466,12 @@
         return buf[...]
 
     share(y1, 0, jnp.concatenate([n_d, s_d, m_d], axis=1))
+    loop(0, nch, lambda c: edge_send(p_o, p_h, 1, c))
     loop(1, nch, send_cot)
+    for side, pole in enumerate((south_pole, north_pole)):
+        pl.when(jnp.logical_not(pole))(lambda: near_copy(side).wait_recv())
     forward_kernel(SECOND)
+    spread_near()
     finish_kernel(SECOND)
     build_forward(w2)
     build_turned(t2)
@@ -436,6 +488,16 @@
     gain, shift, bias = vec[0:1, :], vec[1:2, :], vec[2:3, :]
     center_w, inverse_w = twice(center), twice(inverse)
     gain_w, shift_w, bias_w = twice(gain), twice(shift), twice(bias)
+    inside = [jnp.where(pole, 0.0, 1.0) for pole in (north_pole, south_pole)]
+
+    def edges(row):
+        return jnp.concatenate([row * inside[0], row * inside[1]], axis=1)
+
+    gain_h, shift_h = edges(gain), edges(shift)
+
+    def put_edges(ref, j, c, value):
+        low = value.astype(BF)
+        ref[1 + j, chunk(c), cols_of(0)], ref[1 + j, chunk(c), cols_of(3)] = low[:, :C], low[:, C:]
 
     chip, chips = la // 2, nla // 2
 
@@ -505,9 +567,11 @@
         def one(j, carry):
             normed = (act[j, chunk(c), :] - center_w) * inverse_w
             H[1 + j, chunk(c), own] = (normed * gain_w + shift_w).astype(BF)
+            normed = (act_h[j, chunk(c), :] - center_w) * inverse_w
+            put_edges(H, j, c, normed * gain_h + shift_h)
             return carry
         columns(one, 0)
-        halo_send(H, 1, c)
+        wrap(H, c)
 
     def out_copy(src, dst, ss, rs, c, k):
         m = peer(k)
@@ -565,7 +629,8 @@
     early = min(1, nch - 1)
 
     def second_chunk(c):
-        halo_wait(H, 1, c)
+        first_edge(c)
+        hidden(c)
         received(ct.at[pl.ds(0, Q * (nlo - 1)), chunk(c), :], c_r.at[c])
         conv(taps(H, c), w2)
 
@@ -592,6 +657,7 @@
             g8, s8 = carry
             value = pre[j]
             sg[j, chunk(c), :] = value
+            sg_o[j, chunk(c), :] = value.astype(BF)
             normed = (act[j, chunk(c), :] - center_w) * inverse_w
             return g8 + to_eight(value * normed), s8 + to_eight(value)
 
@@ -599,7 +665,6 @@
         red[1] += g8
         red[2] += s8
 
-    loop(0, nch, hidden)
     def second_step(c):
         second_chunk(c)
         pl.when(c < early)(lambda: send_out(*block_out, c))
@@ -611,6 +676,7 @@
     loop(0, nch, back_chunk)
     sums = [fold(total_row(red[k])) for k in (1, 2, 0)]
     share(y2, 1, jnp.concatenate(sums, axis=1))
+    loop(0, nch, lambda c: edge_send(sg_o, sg_h, 3, c))
     loop(early, nch, lambda c: send_out(*block_out, c))
 
     chip_start(SECOND)
@@ -621,22 +687,36 @@
     shift_part = twice(shift_grad / total)
     gain_part = twice(gain_grad / total)
 
+    scale_h = edges(inverse * gain)
+
+    def act_grad(value, activation, here):
+        normed = (activation - center_w) * inverse_w
+        return value - here * shift_part - here * normed * gain_part
+
     def first_grad(c):
         def one(j, carry):
-            normed = (act[j, chunk(c), :] - center_w) * inverse_w
-            here = cnt[j, chunk(c), :]
-            value = sg[j, chunk(c), :] - here * shift_part - here * normed * gain_part
-            F[1 + j, chunk(c), own] = (scale_w * value * slope[j, chunk(c), :]).astype(BF)
+            grad = act_grad(sg[j, chunk(c), :], act[j, chunk(c), :], cnt[j, chunk(c), :])
+            F[1 + j, chunk(c), own] = (scale_w * grad * slope[j, chunk(c), :]).astype(BF)
             return carry
         columns(one, 0)
-        halo_send(F, 3, c)
+
+    def first_grad_edge(c):
+        edge_wait(sg_h, 3, c)
+
+        def one(j, carry):
+            theirs = sg_h[j, chunk(c), :].astype(F32)
+            grad = act_grad(theirs, act_h[j, chunk(c), :], cnt_h[j, chunk(c), :])
+            put_edges(F, j, c, scale_h * grad * slope_h[j, chunk(c), :])
+            return carry
+        columns(one, 0)
+        wrap(F, c)
 
     def first_kernel(c):
         grad = F[1 : 1 + L, chunk(c), own].reshape(L * CH, W)
         kernel_grad(taps(X, c), grad, acc1)
 
     def field_chunk(c):
-        halo_wait(F, 3, c)
+        first_grad_edge(c)
         out = jnp.dot(taps(F, c), t1[...], preferred_element_type=F32)
         fs[:, chunk(c), :] = out.astype(BF).reshape(L, CH, W)
 
@@ -675,11 +755,15 @@
 
     sent(sb.at[:, pl.ds(1, nlo - 1)], f_s.at[0])
     sent(cb.at[:, pl.ds(1, nlo - 1)], c_s.at[0])
-    sent(wg.at[pl.ds(0, nlo - 1)], wg_s.at[0])
     sent(cm.at[pl.ds(0, nlo - 1)], mask_s.at[0])
-    for h, ref in enumerate((X, H, G, F)):
-        halo_done(ref, h)
+    halo_done(X, 0)
+    edge_done(p_o, 1)
+    halo_done(G, 2)
+    edge_done(sg_o, 3)
+    for side, pole in enumerate((north_pole, south_pole)):
+        pl.when(jnp.logical_not(pole))(lambda: near_copy(side).wait_send())
     for k in range(2):
+        sent(wg.at[k, pl.ds(0, nlo - 1)], wg_s.at[k])
         sent(kg_in.at[k, pl.ds(0, nla // 2 - 1)], kz_s.at[k])
         sent(kg_in.at[k, pl.ds(0, nla // 2)], kc_s.at[k])
         core_copy(k).wait_send()
@@ -762,13 +846,15 @@
         V((Q, B, W), BF), V((Q, B, W), BF), V(flat, BF), V(flat, BF), V(sea.shape, sea.dtype), V(miss.shape, miss.dtype),
         V((1, C), F32), V((1, C), F32), V(wm.shape, F32), V((3, C), F32),
         V((CH * z.PX, C), F32), V((B, z.PX), F32),
-        V((nlo, z.PX, B), F32), wide,
+        V((nlo, z.PX, min(B, 128)), F32), V((nlo, z.PX, min(B, 128)), F32),
+        V((2, nlo, z.PX, min(B, 128)), F32), wide,
         V((nch, nlo, Q, CH, W), BF), V((nch, nlo, Q, CH, W), BF),
         padded, padded, padded, padded, wide, wide, wide,
         V((L, S, W), BF), V((L, CH, W), F32), V((L, S, W), BF), V((L, S, W), BF), V((3, 8, W), F32),
+        V((L, S, W), BF), V((L, S, W), BF), V((L, S, W), BF), V((L, S, W), BF), wide, wide, wide,
         V((12 * C, W), BF), V((12 * C, W), BF), V((12 * C, W), BF), V((12 * C, W), BF),
         V((12 * C, W), F32), V((12 * C, W), F32),
-        V((2, z.wc, z.LP), BF), V((nlo, 2, z.wc, z.LP), BF), V((2, nla, z.wr, C), BF),
+        V((2, z.wc, z.LP), BF), V((2, nlo, z.wc, z.LP), BF), V((2, nla, z.wr, C), BF),
         V((9 * C, C), F32), V((2, z.wr, C), BF),
         V((2, nla // 2, z.wr, C), BF), V((2, nla // 2, z.wr, C), BF),
         V((2, nla // 2, z.wr, C), BF), V((2, nla // 2, z.wr, C), BF), V((2, 9 * C, C), F32),
@@ -776,9 +862,10 @@
         V((n, 1, 3 * C), F32), V((n, 1, 3 * C), F32), V((n, 1, C), F32),
         dma((8,)), dma((1,)), dma((1,)), dma((1,)), dma((nch,)), dma((1,)), dma((nch,)),
         dma((4,)), dma((4, nch)),
-        dma((1,)), dma((nch,)), dma((nch,)), dma((1,)), dma((nch,)), dma((nch,)), dma((1,)), dma((1,)),
+        dma((1,)), dma((nch,)), dma((nch,)), dma((1,)), dma((nch,)), dma((nch,)), dma((2,)), dma((2,)),
         dma((2,)), dma((2,)), dma((2,)), dma((2,)),
         dma((2,)), dma((2,)), dma((2,)), dma((2,)), dma((2,)), dma((2,)), dma((3,)), dma((3,)),
+        dma((2,)), dma((2,)),
     ]
     low, grad, grads = pl.pallas_call(
         functools.partial(main_kernel, z),

time: 74.9 us -> 71.7 us (0.957)
  Pallas kernels: 73.9 us -> 70.8 us
    pallas_call x1, Pallas kernels: 71.8 us -> 68.7 us  [body(): pl.pallas_call(functools.partial(main_kernel, z), out_shape=(V(flat, BF),...]
where the time goes in v4:
time: 71.7 us; the launch traced here: 71.6 us
  Pallas kernels  70.8 us (99%)
  between operations  0.75 us (1%)
    pallas_call x1, Pallas kernels, body(): pl.pallas_call(functools.partial(main_kernel, z), out_shape=(V(flat, BF),...  68.7 us
    pallas_call x1, Pallas kernels, body(): pl.pallas_call(functools.partial(last_kernel, z), out_shape=[shape(flat,...  2.13 us

profile of v4, /device:TPU:0, one launch (start us, length us, event | category | flops | bytes accessed | tf_op | source)
XLA Modules:
  0.0 71.6 jit_solution(267589397407743304)
XLA Ops:
  0.6 0.0 copy-start.3
  0.7 0.0 copy-start.5
  0.7 0.0 copy-start.4
  0.7 0.0 copy-start.2
  0.7 0.0 copy-start.1
  0.7 0.0 copy-start
  0.7 68.7 %block.1 = (bf16[4096,128]{1,0:T(8,128)(2,1)S(1)}, f32[4096,128]{1,0:T(8,128)S(1)}, f32[2,40,256]{2,1,0:T(8,128)S(1)}) custom-call(bf16[4096,128]{1,0:T(8,128)(2,1)} %bitcast.20, bf16[4096,128]{1,0:T(8,128)(2,1)} %bitcast.21, s32[2,4,512]{2,1,0:T(4,128)} %bitcast.22, s32[2,4,512]{2,1,0:T(4,128)} %bitcast.23, f32[1,128]{1,0:T(1,128)} %bitcast.24, ...), custom_call_target="tpu_custom_call" | custom-call | tf_op jit(solution)/shard_map/block/pallas_call | solution.py:870
  69.4 0.0 copy-done.3
  69.4 0.0 copy-done.5
  69.4 0.0 copy-done.4
  69.4 0.0 copy-done.2
  69.4 0.0 copy-done.1
  69.4 0.0 copy-done
  69.4 2.1 %update.1 = (bf16[4096,128]{1,0:T(8,128)(2,1)}, f32[4096,128]{1,0:T(8,128)}, f32[1,1]{1,0:T(1,128)}, f32[2,32,144]{2,1,0:T(8,128)}, f32[2,32,144]{2,1,0:T(8,128)...) custom-call(bf16[4096,128]{1,0:T(8,128)(2,1)S(1)} %get-tuple-element, ...), custom_call_target="tpu_custom_call" | custom-call | tf_op jit(solution)/shard_map/update/pallas_call | solution.py:883
Async XLA Ops:
  0.6 68.7 %copy-start.3 = (f32[3,128]{1,0:T(4,128)S(1)}, f32[3,128]{1,0:T(4,128)}, u32[]{:S(2)}) copy-start(f32[3,128]{1,0:T(4,128)} %vm_h.1) | copy-start | bytes 4612
  0.7 68.7 %copy-start.5 = (f32[3,128]{1,0:T(4,128)S(1)}, f32[3,128]{1,0:T(4,128)}, u32[]{:S(2)}) copy-start(f32[3,128]{1,0:T(4,128)} %vs_h.1) | copy-start | bytes 4612
  0.7 68.7 %copy-start.4 = (f32[3,128]{1,0:T(4,128)S(1)}, f32[3,128]{1,0:T(4,128)}, u32[]{:S(2)}) copy-start(f32[3,128]{1,0:T(4,128)} %vf_h.1) | copy-start | bytes 4612
  0.7 68.7 %copy-start.2 = (f32[2,144,32]{1,2,0:T(8,128)S(1)}, f32[2,144,32]{1,2,0:T(8,128)}, u32[]{:S(2)}) copy-start(f32[2,144,32]{1,2,0:T(8,128)} %param.20) | copy-start | bytes 110596
  0.7 68.7 %copy-start.1 = (f32[2,144,32]{1,2,0:T(8,128)S(1)}, f32[2,144,32]{1,2,0:T(8,128)}, u32[]{:S(2)}) copy-start(f32[2,144,32]{1,2,0:T(8,128)} %param.19) | copy-start | bytes 110596
  0.7 68.7 %copy-start = (f32[2,144,32]{1,2,0:T(8,128)S(1)}, f32[2,144,32]{1,2,0:T(8,128)}, u32[]{:S(2)}) copy-start(f32[2,144,32]{1,2,0:T(8,128)} %param.18) | copy-start | bytes 110596

commit v5 on v4

--- a/solution.py
+++ b/solution.py
@@ -58,10 +58,9 @@
 
 
 def smooth(value):
-    small = jnp.exp(-jnp.abs(value))
-    one = 1.0 + small
-    soft = jnp.maximum(value, 0.0) + jnp.log(one)
-    sigmoid = jnp.where(value >= 0.0, 1.0, small) / one
+    high = 0.5 + 0.5 * jnp.tanh(0.5 * jnp.abs(value))
+    soft = jnp.maximum(value, 0.0) - jnp.log(high)
+    sigmoid = jnp.where(value >= 0.0, high, 1.0 - high)
     return 0.3 * value + 0.7 * soft, 0.3 + 0.7 * sigmoid
 
 
@@ -450,7 +449,7 @@
 
     def first_step(c, stats):
         pl.when(c + 1 < nch)(lambda: arrive(c + 1))
-        pl.when(c + 2 == nch)(lambda: send_cot(0))
+        pl.when(c + 2 == nch)(lambda: loop(0, 2, send_cot))
         return first_chunk(c, stats)
 
     n_d, s_d, m_d = lax.fori_loop(0, nch, first_step, (zero1, zero1, zero1))
@@ -467,7 +466,7 @@
 
     share(y1, 0, jnp.concatenate([n_d, s_d, m_d], axis=1))
     loop(0, nch, lambda c: edge_send(p_o, p_h, 1, c))
-    loop(1, nch, send_cot)
+    loop(2, nch, send_cot)
     for side, pole in enumerate((south_pole, north_pole)):
         pl.when(jnp.logical_not(pole))(lambda: near_copy(side).wait_recv())
     forward_kernel(SECOND)
@@ -626,7 +625,7 @@
 
     block_out = (bo, ob, bo_s, bo_r, bo_o)
     field_out = (fs, fo, fo_s, fo_r, fo_o)
-    early = min(1, nch - 1)
+    early = 2
 
     def second_chunk(c):
         first_edge(c)

time: 71.7 us -> 70.5 us (0.983)
  Pallas kernels: 70.8 us -> 69.6 us
    pallas_call x1, Pallas kernels: 68.7 us -> 67.4 us  [body(): pl.pallas_call(functools.partial(main_kernel, z), out_shape=(V(flat, BF),...]
where the time goes in v5:
time: 70.5 us; the launch traced here: 70.3 us
  Pallas kernels  69.6 us (99%)
  between operations  0.75 us (1%)
    pallas_call x1, Pallas kernels, body(): pl.pallas_call(functools.partial(main_kernel, z), out_shape=(V(flat, BF),...  67.4 us
    pallas_call x1, Pallas kernels, body(): pl.pallas_call(functools.partial(last_kernel, z), out_shape=[shape(flat,...  2.13 us

profile of v5, /device:TPU:0, one launch (start us, length us, event | category | flops | bytes accessed | tf_op | source)
XLA Modules:
  0.0 70.3 jit_solution(2505796023672359323)
XLA Ops:
  0.6 0.0 copy-start.3
  0.7 0.0 copy-start.5
  0.7 0.0 copy-start.4
  0.7 0.0 copy-start.2
  0.7 0.0 copy-start.1
  0.7 0.0 copy-start
  0.7 67.4 %block.1 = (bf16[4096,128]{1,0:T(8,128)(2,1)S(1)}, f32[4096,128]{1,0:T(8,128)S(1)}, f32[2,40,256]{2,1,0:T(8,128)S(1)}) custom-call(bf16[4096,128]{1,0:T(8,128)(2,1)} %bitcast.20, bf16[4096,128]{1,0:T(8,128)(2,1)} %bitcast.21, s32[2,4,512]{2,1,0:T(4,128)} %bitcast.22, s32[2,4,512]{2,1,0:T(4,128)} %bitcast.23, f32[1,128]{1,0:T(1,128)} %bitcast.24, ...), custom_call_target="tpu_custom_call" | custom-call | tf_op jit(solution)/shard_map/block/pallas_call | solution.py:869
  68.2 0.0 copy-done.3
  68.2 0.0 copy-done.5
  68.2 0.0 copy-done.4
  68.2 0.0 copy-done.2
  68.2 0.0 copy-done.1
  68.2 0.0 copy-done
  68.2 2.1 %update.1 = (bf16[4096,128]{1,0:T(8,128)(2,1)}, f32[4096,128]{1,0:T(8,128)}, f32[1,1]{1,0:T(1,128)}, f32[2,32,144]{2,1,0:T(8,128)}, f32[2,32,144]{2,1,0:T(8,128)...) custom-call(bf16[4096,128]{1,0:T(8,128)(2,1)S(1)} %get-tuple-element, ...), custom_call_target="tpu_custom_call" | custom-call | tf_op jit(solution)/shard_map/update/pallas_call | solution.py:882
Async XLA Ops:
  0.6 67.5 %copy-start.3 = (f32[3,128]{1,0:T(4,128)S(1)}, f32[3,128]{1,0:T(4,128)}, u32[]{:S(2)}) copy-start(f32[3,128]{1,0:T(4,128)} %vm_h.1) | copy-start | bytes 4612
  0.7 67.5 %copy-start.5 = (f32[3,128]{1,0:T(4,128)S(1)}, f32[3,128]{1,0:T(4,128)}, u32[]{:S(2)}) copy-start(f32[3,128]{1,0:T(4,128)} %vs_h.1) | copy-start | bytes 4612
  0.7 67.5 %copy-start.4 = (f32[3,128]{1,0:T(4,128)S(1)}, f32[3,128]{1,0:T(4,128)}, u32[]{:S(2)}) copy-start(f32[3,128]{1,0:T(4,128)} %vf_h.1) | copy-start | bytes 4612
  0.7 67.5 %copy-start.2 = (f32[2,144,32]{1,2,0:T(8,128)S(1)}, f32[2,144,32]{1,2,0:T(8,128)}, u32[]{:S(2)}) copy-start(f32[2,144,32]{1,2,0:T(8,128)} %param.20) | copy-start | bytes 110596
  0.7 67.5 %copy-start.1 = (f32[2,144,32]{1,2,0:T(8,128)S(1)}, f32[2,144,32]{1,2,0:T(8,128)}, u32[]{:S(2)}) copy-start(f32[2,144,32]{1,2,0:T(8,128)} %param.19) | copy-start | bytes 110596
  0.7 67.5 %copy-start = (f32[2,144,32]{1,2,0:T(8,128)S(1)}, f32[2,144,32]{1,2,0:T(8,128)}, u32[]{:S(2)}) copy-start(f32[2,144,32]{1,2,0:T(8,128)} %param.18) | copy-start | bytes 110596

commit v6 on v5

--- a/solution.py
+++ b/solution.py
@@ -630,8 +630,8 @@
     def second_chunk(c):
         first_edge(c)
         hidden(c)
+        conv(taps(H, c), w2)
         received(ct.at[pl.ds(0, Q * (nlo - 1)), chunk(c), :], c_r.at[c])
-        conv(taps(H, c), w2)
 
         def one(j, carry):
             value, grad = smooth(pre[j] + bias_w)
@@ -726,10 +726,13 @@
     def field_step(c):
         field_chunk(c)
         pl.when(c < held)(lambda: send_field(c))
-        pl.when(c == 1)(lambda: chip_start(FIRST))
+        pl.when(c == 0)(lambda: chip_start(FIRST))
 
     loop(0, nch, first_grad)
-    loop(0, nch, first_kernel)
+    rows_x = jnp.concatenate([X[b : b + L].reshape(L * S, 4 * C) for b in range(3)], axis=1)
+    acc1[...] = lax.dot_general(
+        rows_x, F[1 : 1 + L, :, own].reshape(L * S, W), (((0,), (0,)), ((), ())), preferred_element_type=F32
+    )
     core_start(FIRST, acc1)
     loop(0, nch, field_step)
     lon_start(SECOND)

time: 70.5 us -> 70 us (level)
  no operation moved by 1% of the time
where the time goes in v6:
time: 70 us; the launch traced here: 69.8 us
  Pallas kernels  69.1 us (99%)
  between operations  0.75 us (1%)
    pallas_call x1, Pallas kernels, body(): pl.pallas_call(functools.partial(main_kernel, z), out_shape=(V(flat, BF),...  66.9 us
    pallas_call x1, Pallas kernels, body(): pl.pallas_call(functools.partial(last_kernel, z), out_shape=[shape(flat,...  2.13 us

profile of v6, /device:TPU:0, one launch (start us, length us, event | category | flops | bytes accessed | tf_op | source)
XLA Modules:
  0.0 69.8 jit_solution(15527521356632932847)
XLA Ops:
  0.6 0.0 copy-start.3
  0.7 0.0 copy-start.5
  0.7 0.0 copy-start.4
  0.7 0.0 copy-start.2
  0.7 0.0 copy-start.1
  0.7 0.0 copy-start
  0.7 66.9 %block.1 = (bf16[4096,128]{1,0:T(8,128)(2,1)S(1)}, f32[4096,128]{1,0:T(8,128)S(1)}, f32[2,40,256]{2,1,0:T(8,128)S(1)}) custom-call(bf16[4096,128]{1,0:T(8,128)(2,1)} %bitcast.20, bf16[4096,128]{1,0:T(8,128)(2,1)} %bitcast.21, s32[2,4,512]{2,1,0:T(4,128)} %bitcast.22, s32[2,4,512]{2,1,0:T(4,128)} %bitcast.23, f32[1,128]{1,0:T(1,128)} %bitcast.24, ...), custom_call_target="tpu_custom_call" | custom-call | tf_op jit(solution)/shard_map/block/pallas_call | solution.py:872
  67.7 0.0 copy-done.3
  67.7 0.0 copy-done.5
  67.7 0.0 copy-done.4
  67.7 0.0 copy-done.2
  67.7 0.0 copy-done.1
  67.7 0.0 copy-done
  67.7 2.1 %update.1 = (bf16[4096,128]{1,0:T(8,128)(2,1)}, f32[4096,128]{1,0:T(8,128)}, f32[1,1]{1,0:T(1,128)}, f32[2,32,144]{2,1,0:T(8,128)}, f32[2,32,144]{2,1,0:T(8,128)...) custom-call(bf16[4096,128]{1,0:T(8,128)(2,1)S(1)} %get-tuple-element, ...), custom_call_target="tpu_custom_call" | custom-call | tf_op jit(solution)/shard_map/update/pallas_call | solution.py:885
Async XLA Ops:
  0.6 67.0 %copy-start.3 = (f32[3,128]{1,0:T(4,128)S(1)}, f32[3,128]{1,0:T(4,128)}, u32[]{:S(2)}) copy-start(f32[3,128]{1,0:T(4,128)} %vm_h.1) | copy-start | bytes 4612
  0.7 67.0 %copy-start.5 = (f32[3,128]{1,0:T(4,128)S(1)}, f32[3,128]{1,0:T(4,128)}, u32[]{:S(2)}) copy-start(f32[3,128]{1,0:T(4,128)} %vs_h.1) | copy-start | bytes 4612
  0.7 67.0 %copy-start.4 = (f32[3,128]{1,0:T(4,128)S(1)}, f32[3,128]{1,0:T(4,128)}, u32[]{:S(2)}) copy-start(f32[3,128]{1,0:T(4,128)} %vf_h.1) | copy-start | bytes 4612
  0.7 67.0 %copy-start.2 = (f32[2,144,32]{1,2,0:T(8,128)S(1)}, f32[2,144,32]{1,2,0:T(8,128)}, u32[]{:S(2)}) copy-start(f32[2,144,32]{1,2,0:T(8,128)} %param.20) | copy-start | bytes 110596
  0.7 67.0 %copy-start.1 = (f32[2,144,32]{1,2,0:T(8,128)S(1)}, f32[2,144,32]{1,2,0:T(8,128)}, u32[]{:S(2)}) copy-start(f32[2,144,32]{1,2,0:T(8,128)} %param.19) | copy-start | bytes 110596
  0.7 67.0 %copy-start = (f32[2,144,32]{1,2,0:T(8,128)S(1)}, f32[2,144,32]{1,2,0:T(8,128)}, u32[]{:S(2)}) copy-start(f32[2,144,32]{1,2,0:T(8,128)} %param.18) | copy-start | bytes 110596

commit v7 on v6

--- a/solution.py
+++ b/solution.py
@@ -76,6 +76,12 @@
         self.nch = self.S // self.CH
         self.wr, self.wc = wrows, wcols
         self.LP = -(-wrows // 128) * 128
+        self.full, self.rest = divmod(wrows, 128)
+        self.shared = self.full > 0 and 0 < 2 * self.rest <= 128
+        each = self.full + (self.rest > 0)
+        self.first = (0, each)
+        self.count = (each, self.full if self.shared else each)
+        self.pieces = sum(self.count)
 
 
 def main_kernel(
@@ -160,13 +166,20 @@
     for k in range(1, nlo):
         cmo[k] = for_lon(peer(k))
     cm[lo] = for_lon(lo)
-    pad = z.LP - z.wr
+    tails = []
     for k in range(2):
         block = wt[k].astype(BF)
-        if pad:
-            block = jnp.concatenate([block, jnp.zeros((z.wc, pad), BF)], axis=1)
-        ws[k] = block
-        wg[k, lo] = block
+        for f in range(z.full):
+            ws[z.first[k] + f] = block[:, f * 128 : (f + 1) * 128]
+        tails.append(block[:, z.full * 128 :])
+    if z.rest:
+        groups = [(z.full, tails)] if z.shared else [(z.first[k] + z.full, tails[k : k + 1]) for k in range(2)]
+        for slot, parts in groups:
+            empty = 128 - z.rest * len(parts)
+            if empty:
+                parts = parts + [jnp.zeros((z.wc, empty), BF)]
+            ws[slot] = jnp.concatenate(parts, axis=1)
+    wg[lo] = ws[...]
     north_pole, south_pole = la == 0, la == nla - 1
     for side, pole in enumerate((north_pole, south_pole)):
         @pl.when(pole)
@@ -178,7 +191,8 @@
             cmn[side] = jnp.zeros_like(cm)
 
     def w_copy(kind, k):
-        return remote(ws.at[kind], wg.at[kind, lo], wg_s.at[kind], wg_r.at[kind], la, peer(k))
+        part = pl.ds(z.first[kind], z.count[kind])
+        return remote(ws.at[part], wg.at[lo, part], wg_s.at[kind], wg_r.at[kind], la, peer(k))
 
     def mask_copy(k):
         return remote(cmo.at[k], cm.at[lo], mask_s.at[0], mask_r.at[0], la, peer(k))
@@ -261,9 +275,16 @@
         return remote(kg_in.at[k, row], kg_in.at[k, row], kc_s.at[k], kc_r.at[k], sibling, lo)
 
     def start_kernel(k):
-        received(wg.at[k, pl.ds(0, nlo - 1)], wg_r.at[k])
-        gathered = jnp.concatenate([wg[k, m].astype(F32) for m in range(nlo)], axis=0)
-        kl[k] = gathered.T[: z.wr].astype(BF)
+        received(wg.at[pl.ds(0, nlo - 1), pl.ds(z.first[k], z.count[k])], wg_r.at[k])
+
+        def turned_block(slot):
+            return jnp.concatenate([wg[m, slot].astype(F32) for m in range(nlo)], axis=0).T.astype(BF)
+
+        for f in range(z.full):
+            kl[k, f * 128 : (f + 1) * 128] = turned_block(z.first[k] + f)
+        if z.rest:
+            slot, start = (z.full, k * z.rest) if z.shared else (z.first[k] + z.full, 0)
+            kl[k, z.full * 128 : z.wr] = turned_block(slot)[start : start + z.rest]
         kg_in[k, la] = kl[k]
         loop(1, nla // 2, lambda d: kz_copy(k, d).start())
         kc_copy(k, 0).start()
@@ -765,7 +786,7 @@
     for side, pole in enumerate((north_pole, south_pole)):
         pl.when(jnp.logical_not(pole))(lambda: near_copy(side).wait_send())
     for k in range(2):
-        sent(wg.at[k, pl.ds(0, nlo - 1)], wg_s.at[k])
+        sent(wg.at[pl.ds(0, nlo - 1), pl.ds(z.first[k], z.count[k])], wg_s.at[k])
         sent(kg_in.at[k, pl.ds(0, nla // 2 - 1)], kz_s.at[k])
         sent(kg_in.at[k, pl.ds(0, nla // 2)], kc_s.at[k])
         core_copy(k).wait_send()
@@ -856,7 +877,7 @@
         V((L, S, W), BF), V((L, S, W), BF), V((L, S, W), BF), V((L, S, W), BF), wide, wide, wide,
         V((12 * C, W), BF), V((12 * C, W), BF), V((12 * C, W), BF), V((12 * C, W), BF),
         V((12 * C, W), F32), V((12 * C, W), F32),
-        V((2, z.wc, z.LP), BF), V((2, nlo, z.wc, z.LP), BF), V((2, nla, z.wr, C), BF),
+        V((z.pieces, z.wc, 128), BF), V((nlo, z.pieces, z.wc, 128), BF), V((2, nla, z.wr, C), BF),
         V((9 * C, C), F32), V((2, z.wr, C), BF),
         V((2, nla // 2, z.wr, C), BF), V((2, nla // 2, z.wr, C), BF),
         V((2, nla // 2, z.wr, C), BF), V((2, nla // 2, z.wr, C), BF), V((2, 9 * C, C), F32),

time: 70 us -> 69.9 us (level)
  no operation moved by 1% of the time
where the time goes in v7:
time: 69.9 us; the launch traced here: 69.8 us
  Pallas kernels  69 us (99%)
  between operations  0.75 us (1%)
    pallas_call x1, Pallas kernels, body(): pl.pallas_call(functools.partial(main_kernel, z), out_shape=(V(flat, BF),...  66.9 us
    pallas_call x1, Pallas kernels, body(): pl.pallas_call(functools.partial(last_kernel, z), out_shape=[shape(flat,...  2.13 us

profile of v7, /device:TPU:0, one launch (start us, length us, event | category | flops | bytes accessed | tf_op | source)
XLA Modules:
  0.0 69.8 jit_solution(12657784677655138530)
XLA Ops:
  0.6 0.0 copy-start.3
  0.7 0.0 copy-start.5
  0.7 0.0 copy-start.4
  0.7 0.0 copy-start.2
  0.7 0.0 copy-start.1
  0.7 0.0 copy-start
  0.7 66.9 %block.1 = (bf16[4096,128]{1,0:T(8,128)(2,1)S(1)}, f32[4096,128]{1,0:T(8,128)S(1)}, f32[2,40,256]{2,1,0:T(8,128)S(1)}) custom-call(bf16[4096,128]{1,0:T(8,128)(2,1)} %bitcast.20, bf16[4096,128]{1,0:T(8,128)(2,1)} %bitcast.21, s32[2,4,512]{2,1,0:T(4,128)} %bitcast.22, s32[2,4,512]{2,1,0:T(4,128)} %bitcast.23, f32[1,128]{1,0:T(1,128)} %bitcast.24, ...), custom_call_target="tpu_custom_call" | custom-call | tf_op jit(solution)/shard_map/block/pallas_call | solution.py:893
  67.6 0.0 copy-done.3
  67.6 0.0 copy-done.5
  67.6 0.0 copy-done.4
  67.6 0.0 copy-done.2
  67.6 0.0 copy-done.1
  67.6 0.0 copy-done
  67.7 2.1 %update.1 = (bf16[4096,128]{1,0:T(8,128)(2,1)}, f32[4096,128]{1,0:T(8,128)}, f32[1,1]{1,0:T(1,128)}, f32[2,32,144]{2,1,0:T(8,128)}, f32[2,32,144]{2,1,0:T(8,128)...) custom-call(bf16[4096,128]{1,0:T(8,128)(2,1)S(1)} %get-tuple-element, ...), custom_call_target="tpu_custom_call" | custom-call | tf_op jit(solution)/shard_map/update/pallas_call | solution.py:906
Async XLA Ops:
  0.6 67.0 %copy-start.3 = (f32[3,128]{1,0:T(4,128)S(1)}, f32[3,128]{1,0:T(4,128)}, u32[]{:S(2)}) copy-start(f32[3,128]{1,0:T(4,128)} %vm_h.1) | copy-start | bytes 4612
  0.7 67.0 %copy-start.5 = (f32[3,128]{1,0:T(4,128)S(1)}, f32[3,128]{1,0:T(4,128)}, u32[]{:S(2)}) copy-start(f32[3,128]{1,0:T(4,128)} %vs_h.1) | copy-start | bytes 4612
  0.7 67.0 %copy-start.4 = (f32[3,128]{1,0:T(4,128)S(1)}, f32[3,128]{1,0:T(4,128)}, u32[]{:S(2)}) copy-start(f32[3,128]{1,0:T(4,128)} %vf_h.1) | copy-start | bytes 4612
  0.7 67.0 %copy-start.2 = (f32[2,144,32]{1,2,0:T(8,128)S(1)}, f32[2,144,32]{1,2,0:T(8,128)}, u32[]{:S(2)}) copy-start(f32[2,144,32]{1,2,0:T(8,128)} %param.20) | copy-start | bytes 110596
  0.7 67.0 %copy-start.1 = (f32[2,144,32]{1,2,0:T(8,128)S(1)}, f32[2,144,32]{1,2,0:T(8,128)}, u32[]{:S(2)}) copy-start(f32[2,144,32]{1,2,0:T(8,128)} %param.19) | copy-start | bytes 110596
  0.7 67.0 %copy-start = (f32[2,144,32]{1,2,0:T(8,128)S(1)}, f32[2,144,32]{1,2,0:T(8,128)}, u32[]{:S(2)}) copy-start(f32[2,144,32]{1,2,0:T(8,128)} %param.18) | copy-start | bytes 110596

commit v8 on v7

--- a/solution.py
+++ b/solution.py
@@ -646,7 +646,7 @@
 
     block_out = (bo, ob, bo_s, bo_r, bo_o)
     field_out = (fs, fo, fo_s, fo_r, fo_o)
-    early = 2
+    early = 3
 
     def second_chunk(c):
         first_edge(c)

time: 69.9 us -> 70 us (level)
  no operation moved by 1% of the time
where the time goes in v8:
time: 70 us; the launch traced here: 69.8 us
  Pallas kernels  69.1 us (99%)
  between operations  0.75 us (1%)
    pallas_call x1, Pallas kernels, body(): pl.pallas_call(functools.partial(main_kernel, z), out_shape=(V(flat, BF),...  66.9 us
    pallas_call x1, Pallas kernels, body(): pl.pallas_call(functools.partial(last_kernel, z), out_shape=[shape(flat,...  2.13 us

profile of v8, /device:TPU:0, one launch (start us, length us, event | category | flops | bytes accessed | tf_op | source)
XLA Modules:
  0.0 69.8 jit_solution(1964131202494274293)
XLA Ops:
  0.6 0.0 copy-start.3
  0.7 0.0 copy-start.5
  0.7 0.0 copy-start.4
  0.7 0.0 copy-start.2
  0.7 0.0 copy-start.1
  0.7 0.0 copy-start
  0.7 66.9 %block.1 = (bf16[4096,128]{1,0:T(8,128)(2,1)S(1)}, f32[4096,128]{1,0:T(8,128)S(1)}, f32[2,40,256]{2,1,0:T(8,128)S(1)}) custom-call(bf16[4096,128]{1,0:T(8,128)(2,1)} %bitcast.20, bf16[4096,128]{1,0:T(8,128)(2,1)} %bitcast.21, s32[2,4,512]{2,1,0:T(4,128)} %bitcast.22, s32[2,4,512]{2,1,0:T(4,128)} %bitcast.23, f32[1,128]{1,0:T(1,128)} %bitcast.24, ...), custom_call_target="tpu_custom_call" | custom-call | tf_op jit(solution)/shard_map/block/pallas_call | solution.py:893
  67.7 0.0 copy-done.3
  67.7 0.0 copy-done.5
  67.7 0.0 copy-done.4
  67.7 0.0 copy-done.2
  67.7 0.0 copy-done.1
  67.7 0.0 copy-done
  67.7 2.1 %update.1 = (bf16[4096,128]{1,0:T(8,128)(2,1)}, f32[4096,128]{1,0:T(8,128)}, f32[1,1]{1,0:T(1,128)}, f32[2,32,144]{2,1,0:T(8,128)}, f32[2,32,144]{2,1,0:T(8,128)...) custom-call(bf16[4096,128]{1,0:T(8,128)(2,1)S(1)} %get-tuple-element, ...), custom_call_target="tpu_custom_call" | custom-call | tf_op jit(solution)/shard_map/update/pallas_call | solution.py:906
Async XLA Ops:
  0.6 67.0 %copy-start.3 = (f32[3,128]{1,0:T(4,128)S(1)}, f32[3,128]{1,0:T(4,128)}, u32[]{:S(2)}) copy-start(f32[3,128]{1,0:T(4,128)} %vm_h.1) | copy-start | bytes 4612
  0.7 67.0 %copy-start.5 = (f32[3,128]{1,0:T(4,128)S(1)}, f32[3,128]{1,0:T(4,128)}, u32[]{:S(2)}) copy-start(f32[3,128]{1,0:T(4,128)} %vs_h.1) | copy-start | bytes 4612
  0.7 67.0 %copy-start.4 = (f32[3,128]{1,0:T(4,128)S(1)}, f32[3,128]{1,0:T(4,128)}, u32[]{:S(2)}) copy-start(f32[3,128]{1,0:T(4,128)} %vf_h.1) | copy-start | bytes 4612
  0.7 67.0 %copy-start.2 = (f32[2,144,32]{1,2,0:T(8,128)S(1)}, f32[2,144,32]{1,2,0:T(8,128)}, u32[]{:S(2)}) copy-start(f32[2,144,32]{1,2,0:T(8,128)} %param.20) | copy-start | bytes 110596
  0.7 67.0 %copy-start.1 = (f32[2,144,32]{1,2,0:T(8,128)S(1)}, f32[2,144,32]{1,2,0:T(8,128)}, u32[]{:S(2)}) copy-start(f32[2,144,32]{1,2,0:T(8,128)} %param.19) | copy-start | bytes 110596
  0.7 67.0 %copy-start = (f32[2,144,32]{1,2,0:T(8,128)S(1)}, f32[2,144,32]{1,2,0:T(8,128)}, u32[]{:S(2)}) copy-start(f32[2,144,32]{1,2,0:T(8,128)} %param.18) | copy-start | bytes 110596
